TPU v7x, 128 devices: a whole 4x4x4 slice. The times are simulated.
128 devices in a mesh: tm: 8 (over y, core), space: 16 (over z, x).
Axes of the slice: x: 4, y: 4, z: 4, core: 2. Of those that a mesh axis runs over, the one named last changes fastest.
Arguments:
- dinv: bfloat16 [8, 1024, 1024], P('tm', 'space')
- coupling: bfloat16 [8, 1024, 1024], P('tm'), may hold values from -0.15625 to 0.15625
- owner_position: int32 [1024], P('space'), may hold values from 0 to 1023, as said below
- pattern: int32 [16, 4], P('space'), may hold values from 0 to 7, all different within a row
- basis: bfloat16 [1024, 512], replicated, may hold values from -0.25 to 0.25
Outputs:
- sigma: bfloat16 [8, 1024, 1024], P('tm', 'space')
- gradient: bfloat16 [8, 1024, 512], P('tm', 'space')
Inputs may be any that keep to these rules, and one draw needn't show every extreme that they name: `owner_position`: A permutation; the rows of space device j (rows j*64 to (j+1)*64 - 1) take exactly 4 positions in each aligned block of 64 positions, namely positions o*64 + j*4 to o*64 + (j+1)*4 - 1. `pattern`: each row names 4 different blocks.
All inputs are finite; a program needn't handle non-finite values.
Results may differ from a plain program's by a relative error of at most 0.022.
Values may be sent and summed in bfloat16 or wider, within the bound.
A program may use at most 64 MiB of HBM per device.

v0:
```python
import jax
import jax.numpy as jnp
from jax import lax
from jax.sharding import PartitionSpec as P


def shifted(value, axis, steps):
    count = lax.axis_size(axis)
    leading, last = (max(0, -steps), min(count, count - steps))
    return lax.ppermute(value, axis, [(source, source + steps) for source in range(leading, last)])


def on_device(dinv, coupling, owner_position, pattern, basis):
    local_steps = coupling.shape[0]
    block_width = coupling.shape[1]
    row_count = dinv.shape[1]
    spaces = lax.axis_size("space")
    first_row = lax.axis_index("space") * row_count
    own_coupling = lax.dynamic_slice_in_dim(coupling, first_row, row_count, 1)

    def one_turn(turn_index, state_pair):
        incoming, previous = state_pair
        carried = incoming
        sigma_rows = [None] * local_steps
        gathered = lax.all_gather(carried, "space", axis=0, tiled=True)
        product_rows = jnp.dot(own_coupling[0], gathered, preferred_element_type=jnp.float32)
        product_rows = product_rows.astype(jnp.bfloat16)
        current = dinv[0].astype(jnp.float32) + lax.dot_general(
            product_rows, coupling[0], (((1,), (1,)), ((), ())), preferred_element_type=jnp.float32
        )
        sigma_rows[0] = current
        carried = current.astype(jnp.bfloat16)
        passed = shifted(carried, "tm", -1)
        return (passed, jnp.stack(sigma_rows))

    start_state = (
        jnp.zeros((row_count, block_width), jnp.bfloat16),
        jnp.zeros((local_steps, row_count, block_width), jnp.float32),
    )
    final_state = lax.fori_loop(0, lax.axis_size("tm"), one_turn, start_state)
    sigma_out = final_state[1].astype(jnp.bfloat16)
    pair_rows = row_count // spaces
    target = owner_position // row_count * pair_rows + owner_position % pair_rows
    slots = jnp.arange(row_count, dtype=jnp.int32)
    placement_table = (slots[:, None] == target[None, :]).astype(jnp.bfloat16)
    ordered = jnp.einsum(
        "ql,tlc->qtc", placement_table, sigma_out, preferred_element_type=jnp.float32
    ).astype(jnp.bfloat16)
    pieces = [lax.all_to_all(ordered[:, 0, :], "space", split_axis=0, concat_axis=0, tiled=True)]
    received = jnp.stack(pieces, axis=1)
    column_block = jnp.arange(block_width, dtype=jnp.int32) // 128
    selected = jnp.any(pattern[0][:, None] == column_block[None, :], axis=0).astype(jnp.bfloat16)
    masked = received * selected[None, None, :]
    gradient = jnp.einsum("rtc,ch->trh", masked, basis, preferred_element_type=jnp.float32)
    return (sigma_out, gradient.astype(jnp.bfloat16))


def solution(mesh):
    placed = (P("tm", "space", None), P("tm", None, None), P("space"), P("space", None), P())
    return jax.shard_map(
        on_device,
        mesh=mesh,
        in_specs=placed,
        out_specs=(P("tm", "space", None), P("tm", "space", None)),
        check_vma=False,
    )
```

profile of v0, /device:TPU:1, one launch (start us, length us, event | category | flops | bytes accessed | tf_op | source)
XLA Modules:
  0.0 489.7 jit_solution(1296490223757740988)
XLA Ops:
  8.9 459.7 %while.12 = (s32[]{:T(128)}, bf16[64,1024]{1,0:T(8,128)(2,1)S(1)}, bf16[1,64,1024]{2,1,0:T(8,128)(2,1)}, bf16[1,64,1024]{2,1,0:T(8,128)(2,1)}, bf16[1,64,1024]{2...) while((s32[]{:T(128)}, bf16[64,1024]{1,0:T(8,128)(2,1)S(1)}, ...), condition=%wide.region_1.0_spmd, body=%wide.region_0.0_spmd.sunk | while | flops 268697600 | bytes 12845269 | solution.py:40
  9.7 50.3 %all-gather.2.cloned.1.call-done = bf16[1024,1024]{1,0:T(8,128)(2,1)} async-done(((bf16[64,1024]{1,0:T(8,128)(2,1)}), bf16[1024,1024]{1,0:T(8,128)(2,1)}) %all-gather.2.cloned.1.call-update) | async-done | bytes 2097168 | tf_op jit(solution)/shard_map/while/body/eval_jaxpr/all_gather | solution.py:25
  63.3 3.6 collective-permute-start
  66.9 3.7 collective-permute-done
  71.4 45.5 %all-gather.2.cloned.1.call-done = bf16[1024,1024]{1,0:T(8,128)(2,1)} async-done(((bf16[64,1024]{1,0:T(8,128)(2,1)}), bf16[1024,1024]{1,0:T(8,128)(2,1)}) %all-gather.2.cloned.1.call-update) | async-done | bytes 2097168 | tf_op jit(solution)/shard_map/while/body/eval_jaxpr/all_gather | solution.py:25
  116.9 3.4 fusion.25
  120.3 3.6 collective-permute-start
  123.9 3.7 collective-permute-done
  128.4 45.5 %all-gather.2.cloned.1.call-done = bf16[1024,1024]{1,0:T(8,128)(2,1)} async-done(((bf16[64,1024]{1,0:T(8,128)(2,1)}), bf16[1024,1024]{1,0:T(8,128)(2,1)}) %all-gather.2.cloned.1.call-update) | async-done | bytes 2097168 | tf_op jit(solution)/shard_map/while/body/eval_jaxpr/all_gather | solution.py:25
  173.9 3.4 fusion.25
  177.2 3.6 collective-permute-start
  180.9 3.7 collective-permute-done
  185.3 45.2 %all-gather.2.cloned.1.call-done = bf16[1024,1024]{1,0:T(8,128)(2,1)} async-done(((bf16[64,1024]{1,0:T(8,128)(2,1)}), bf16[1024,1024]{1,0:T(8,128)(2,1)}) %all-gather.2.cloned.1.call-update) | async-done | bytes 2097168 | tf_op jit(solution)/shard_map/while/body/eval_jaxpr/all_gather | solution.py:25
  230.5 3.3 fusion.25
  233.9 3.6 collective-permute-start
  237.5 3.7 collective-permute-done
  242.0 45.2 %all-gather.2.cloned.1.call-done = bf16[1024,1024]{1,0:T(8,128)(2,1)} async-done(((bf16[64,1024]{1,0:T(8,128)(2,1)}), bf16[1024,1024]{1,0:T(8,128)(2,1)}) %all-gather.2.cloned.1.call-update) | async-done | bytes 2097168 | tf_op jit(solution)/shard_map/while/body/eval_jaxpr/all_gather | solution.py:25
  287.2 3.4 fusion.25
  290.6 3.6 collective-permute-start
  294.2 3.7 collective-permute-done
  298.6 45.2 %all-gather.2.cloned.1.call-done = bf16[1024,1024]{1,0:T(8,128)(2,1)} async-done(((bf16[64,1024]{1,0:T(8,128)(2,1)}), bf16[1024,1024]{1,0:T(8,128)(2,1)}) %all-gather.2.cloned.1.call-update) | async-done | bytes 2097168 | tf_op jit(solution)/shard_map/while/body/eval_jaxpr/all_gather | solution.py:25
  343.9 3.4 fusion.25
  347.2 3.6 collective-permute-start
  350.9 3.7 collective-permute-done
  355.3 45.5 %all-gather.2.cloned.1.call-done = bf16[1024,1024]{1,0:T(8,128)(2,1)} async-done(((bf16[64,1024]{1,0:T(8,128)(2,1)}), bf16[1024,1024]{1,0:T(8,128)(2,1)}) %all-gather.2.cloned.1.call-update) | async-done | bytes 2097168 | tf_op jit(solution)/shard_map/while/body/eval_jaxpr/all_gather | solution.py:25
  404.2 3.6 collective-permute-start
  407.9 3.7 collective-permute-done
  412.3 45.5 %all-gather.2.cloned.1.call-done = bf16[1024,1024]{1,0:T(8,128)(2,1)} async-done(((bf16[64,1024]{1,0:T(8,128)(2,1)}), bf16[1024,1024]{1,0:T(8,128)(2,1)}) %all-gather.2.cloned.1.call-update) | async-done | bytes 2097168 | tf_op jit(solution)/shard_map/while/body/eval_jaxpr/all_gather | solution.py:25
  461.2 3.6 collective-permute-start
  464.8 3.7 collective-permute-done
  470.3 4.7 all-to-all-start
  475.1 6.7 %all-to-all-done = bf16[16,4,1024]{2,1,0:T(4,128)(2,1)S(1)} async-done(((bf16[16,4,1024]{2,1,0:T(4,128)(2,1)}), bf16[16,4,1024]{2,1,0:T(4,128)(2,1)S(1)}, u32[]{:S(2)}, u32[]{:S(2)}) %all-to-all-start) | async-done | bytes 131104 | tf_op jit(solution)/shard_map/all_to_all | solution.py:49
  (66 shorter events, 20.3 us)
Async XLA Ops:
  7.2 474.7 %copy-start = (bf16[1024,512]{1,0:T(8,128)(2,1)S(1)}, bf16[1024,512]{1,0:T(8,128)(2,1)}, u32[]{:S(2)}) copy-start(bf16[1024,512]{1,0:T(8,128)(2,1)} %param.11) | copy-start | bytes 3145732
  8.9 466.1 %copy-start.3 = (s32[1,4]{1,0:T(1,128)S(1)}, s32[1,4]{1,0:T(1,128)}, u32[]{:S(2)}) copy-start(s32[1,4]{1,0:T(1,128)} %param.10) | copy-start | bytes 52
  8.9 0.7 copy-start.1
  8.9 51.0 %all-gather.2.cloned.1.call-start = ((), (), s32[]{:S(2)}) async-start(), calls=%async_computation.1 | async-start | bytes 2228224 | tf_op jit(solution)/shard_map/while/body/eval_jaxpr/all_gather | solution.py:25
  63.3 7.4 %copy-start.2 = (bf16[64,1024]{1,0:T(8,128)(2,1)}, bf16[64,1024]{1,0:T(8,128)(2,1)S(1)}, u32[]{:S(2)}) copy-start(bf16[64,1024]{1,0:T(8,128)(2,1)S(1)} %fusion.25) | copy-start | bytes 393220 | tf_op jit(solution)/shard_map/while
  63.3 7.4 %collective-permute-start = (bf16[64,1024]{1,0:T(8,128)(2,1)S(1)}, bf16[64,1024]{1,0:T(8,128)(2,1)S(1)}, u32[]{:S(2)}, u32[]{:S(2)}) collective-permute-start(bf16[64,1024]{1,0:T(8,128)(2,1)S(1)} %fusion.25), channel_id=1, source_target_pairs={{16,0},{32,16},{48,32},{64,48},{80,64},{96,80},{112,96},{17,1},{33... | collective-permute-start | bytes 393224 | tf_op jit(solution)/shard_map/while/body/eval_jaxpr/ppermute | solution.py:10
  70.7 0.7 copy-start.1
  70.7 46.2 %all-gather.2.cloned.1.call-start = ((), (), s32[]{:S(2)}) async-start(), calls=%async_computation.1 | async-start | bytes 2228224 | tf_op jit(solution)/shard_map/while/body/eval_jaxpr/all_gather | solution.py:25
  120.3 7.4 %copy-start.2 = (bf16[64,1024]{1,0:T(8,128)(2,1)}, bf16[64,1024]{1,0:T(8,128)(2,1)S(1)}, u32[]{:S(2)}) copy-start(bf16[64,1024]{1,0:T(8,128)(2,1)S(1)} %fusion.25) | copy-start | bytes 393220 | tf_op jit(solution)/shard_map/while
  120.3 7.4 %collective-permute-start = (bf16[64,1024]{1,0:T(8,128)(2,1)S(1)}, bf16[64,1024]{1,0:T(8,128)(2,1)S(1)}, u32[]{:S(2)}, u32[]{:S(2)}) collective-permute-start(bf16[64,1024]{1,0:T(8,128)(2,1)S(1)} %fusion.25), channel_id=1, source_target_pairs={{16,0},{32,16},{48,32},{64,48},{80,64},{96,80},{112,96},{17,1},{33... | collective-permute-start | bytes 393224 | tf_op jit(solution)/shard_map/while/body/eval_jaxpr/ppermute | solution.py:10
  127.6 0.7 copy-start.1
  127.6 46.2 %all-gather.2.cloned.1.call-start = ((), (), s32[]{:S(2)}) async-start(), calls=%async_computation.1 | async-start | bytes 2228224 | tf_op jit(solution)/shard_map/while/body/eval_jaxpr/all_gather | solution.py:25
  177.2 7.4 %copy-start.2 = (bf16[64,1024]{1,0:T(8,128)(2,1)}, bf16[64,1024]{1,0:T(8,128)(2,1)S(1)}, u32[]{:S(2)}) copy-start(bf16[64,1024]{1,0:T(8,128)(2,1)S(1)} %fusion.25) | copy-start | bytes 393220 | tf_op jit(solution)/shard_map/while
  177.2 7.4 %collective-permute-start = (bf16[64,1024]{1,0:T(8,128)(2,1)S(1)}, bf16[64,1024]{1,0:T(8,128)(2,1)S(1)}, u32[]{:S(2)}, u32[]{:S(2)}) collective-permute-start(bf16[64,1024]{1,0:T(8,128)(2,1)S(1)} %fusion.25), channel_id=1, source_target_pairs={{16,0},{32,16},{48,32},{64,48},{80,64},{96,80},{112,96},{17,1},{33... | collective-permute-start | bytes 393224 | tf_op jit(solution)/shard_map/while/body/eval_jaxpr/ppermute | solution.py:10
  184.6 45.9 %all-gather.2.cloned.1.call-start = ((), (), s32[]{:S(2)}) async-start(), calls=%async_computation.1 | async-start | bytes 2228224 | tf_op jit(solution)/shard_map/while/body/eval_jaxpr/all_gather | solution.py:25
  233.9 7.4 %copy-start.2 = (bf16[64,1024]{1,0:T(8,128)(2,1)}, bf16[64,1024]{1,0:T(8,128)(2,1)S(1)}, u32[]{:S(2)}) copy-start(bf16[64,1024]{1,0:T(8,128)(2,1)S(1)} %fusion.25) | copy-start | bytes 393220 | tf_op jit(solution)/shard_map/while
  233.9 7.4 %collective-permute-start = (bf16[64,1024]{1,0:T(8,128)(2,1)S(1)}, bf16[64,1024]{1,0:T(8,128)(2,1)S(1)}, u32[]{:S(2)}, u32[]{:S(2)}) collective-permute-start(bf16[64,1024]{1,0:T(8,128)(2,1)S(1)} %fusion.25), channel_id=1, source_target_pairs={{16,0},{32,16},{48,32},{64,48},{80,64},{96,80},{112,96},{17,1},{33... | collective-permute-start | bytes 393224 | tf_op jit(solution)/shard_map/while/body/eval_jaxpr/ppermute | solution.py:10
  241.3 0.7 copy-start.1
  241.3 45.9 %all-gather.2.cloned.1.call-start = ((), (), s32[]{:S(2)}) async-start(), calls=%async_computation.1 | async-start | bytes 2228224 | tf_op jit(solution)/shard_map/while/body/eval_jaxpr/all_gather | solution.py:25
  290.6 7.4 %copy-start.2 = (bf16[64,1024]{1,0:T(8,128)(2,1)}, bf16[64,1024]{1,0:T(8,128)(2,1)S(1)}, u32[]{:S(2)}) copy-start(bf16[64,1024]{1,0:T(8,128)(2,1)S(1)} %fusion.25) | copy-start | bytes 393220 | tf_op jit(solution)/shard_map/while
  290.6 7.4 %collective-permute-start = (bf16[64,1024]{1,0:T(8,128)(2,1)S(1)}, bf16[64,1024]{1,0:T(8,128)(2,1)S(1)}, u32[]{:S(2)}, u32[]{:S(2)}) collective-permute-start(bf16[64,1024]{1,0:T(8,128)(2,1)S(1)} %fusion.25), channel_id=1, source_target_pairs={{16,0},{32,16},{48,32},{64,48},{80,64},{96,80},{112,96},{17,1},{33... | collective-permute-start | bytes 393224 | tf_op jit(solution)/shard_map/while/body/eval_jaxpr/ppermute | solution.py:10
  297.9 0.7 copy-start.1
  297.9 45.9 %all-gather.2.cloned.1.call-start = ((), (), s32[]{:S(2)}) async-start(), calls=%async_computation.1 | async-start | bytes 2228224 | tf_op jit(solution)/shard_map/while/body/eval_jaxpr/all_gather | solution.py:25
  347.2 7.4 %copy-start.2 = (bf16[64,1024]{1,0:T(8,128)(2,1)}, bf16[64,1024]{1,0:T(8,128)(2,1)S(1)}, u32[]{:S(2)}) copy-start(bf16[64,1024]{1,0:T(8,128)(2,1)S(1)} %fusion.25) | copy-start | bytes 393220 | tf_op jit(solution)/shard_map/while
  347.2 7.4 %collective-permute-start = (bf16[64,1024]{1,0:T(8,128)(2,1)S(1)}, bf16[64,1024]{1,0:T(8,128)(2,1)S(1)}, u32[]{:S(2)}, u32[]{:S(2)}) collective-permute-start(bf16[64,1024]{1,0:T(8,128)(2,1)S(1)} %fusion.25), channel_id=1, source_target_pairs={{16,0},{32,16},{48,32},{64,48},{80,64},{96,80},{112,96},{17,1},{33... | collective-permute-start | bytes 393224 | tf_op jit(solution)/shard_map/while/body/eval_jaxpr/ppermute | solution.py:10
  354.6 46.2 %all-gather.2.cloned.1.call-start = ((), (), s32[]{:S(2)}) async-start(), calls=%async_computation.1 | async-start | bytes 2228224 | tf_op jit(solution)/shard_map/while/body/eval_jaxpr/all_gather | solution.py:25
  404.2 7.4 %copy-start.2 = (bf16[64,1024]{1,0:T(8,128)(2,1)}, bf16[64,1024]{1,0:T(8,128)(2,1)S(1)}, u32[]{:S(2)}) copy-start(bf16[64,1024]{1,0:T(8,128)(2,1)S(1)} %fusion.25) | copy-start | bytes 393220 | tf_op jit(solution)/shard_map/while
  404.2 7.4 %collective-permute-start = (bf16[64,1024]{1,0:T(8,128)(2,1)S(1)}, bf16[64,1024]{1,0:T(8,128)(2,1)S(1)}, u32[]{:S(2)}, u32[]{:S(2)}) collective-permute-start(bf16[64,1024]{1,0:T(8,128)(2,1)S(1)} %fusion.25), channel_id=1, source_target_pairs={{16,0},{32,16},{48,32},{64,48},{80,64},{96,80},{112,96},{17,1},{33... | collective-permute-start | bytes 393224 | tf_op jit(solution)/shard_map/while/body/eval_jaxpr/ppermute | solution.py:10
  411.6 46.2 %all-gather.2.cloned.1.call-start = ((), (), s32[]{:S(2)}) async-start(), calls=%async_computation.1 | async-start | bytes 2228224 | tf_op jit(solution)/shard_map/while/body/eval_jaxpr/all_gather | solution.py:25
  461.2 7.4 %copy-start.2 = (bf16[64,1024]{1,0:T(8,128)(2,1)}, bf16[64,1024]{1,0:T(8,128)(2,1)S(1)}, u32[]{:S(2)}) copy-start(bf16[64,1024]{1,0:T(8,128)(2,1)S(1)} %fusion.25) | copy-start | bytes 393220 | tf_op jit(solution)/shard_map/while
  461.2 7.4 %collective-permute-start = (bf16[64,1024]{1,0:T(8,128)(2,1)S(1)}, bf16[64,1024]{1,0:T(8,128)(2,1)S(1)}, u32[]{:S(2)}, u32[]{:S(2)}) collective-permute-start(bf16[64,1024]{1,0:T(8,128)(2,1)S(1)} %fusion.25), channel_id=1, source_target_pairs={{16,0},{32,16},{48,32},{64,48},{80,64},{96,80},{112,96},{17,1},{33... | collective-permute-start | bytes 393224 | tf_op jit(solution)/shard_map/while/body/eval_jaxpr/ppermute | solution.py:10
  470.3 11.5 %all-to-all-start = ((bf16[16,4,1024]{2,1,0:T(4,128)(2,1)}), bf16[16,4,1024]{2,1,0:T(4,128)(2,1)S(1)}, u32[]{:S(2)}, u32[]{:S(2)}) async-start(bf16[16,4,1024]{2,1,0:T(4,128)(2,1)} %all_to_all.8), calls=%async_computation | async-start | bytes 262144 | tf_op jit(solution)/shard_map/all_to_all | solution.py:49
  (3 other events, 2.0 us)
Sparse Core Ops, SparseCore 0:
  12.5 47.4 all-gather.1
  74.2 42.6 all-gather.1
  131.2 42.6 all-gather.1
  187.8 42.6 all-gather.1
  244.5 42.6 all-gather.1
  301.2 42.6 all-gather.1
  358.1 42.6 all-gather.1
  415.1 42.6 all-gather.1
where the time goes:
time: 490 us
  waiting for transfers between devices  405 us (83%)
  starting transfers between devices  33.8 us (7%)
  matrix products  28.8 us (6%)
  between operations  14.1 us (3%)
  local copies, waits for them, and re-layouts  6.89 us (1%)
    all_gather x8, waiting for transfers between devices, one_turn(): gathered = lax.all_gather(carried, 'space', axis=0, tiled=True)  368 us
    ppermute x8, waiting for transfers between devices, shifted(): lax.ppermute(value, axis, [(source, source + steps) for source in range(l...  29.8 us
    ppermute x8, starting transfers between devices, shifted(): lax.ppermute(value, axis, [(source, source + steps) for source in range(l...  29.1 us
    dot_general x8, matrix products, one_turn(): lax.dot_general(product_rows, coupling[0], (((1,), (1,)), ((), ())), pref...  26.8 us
  transfers between devices with their start and end apart: 17, of which 17 were waited for; matrix products, arithmetic and copies ran while one was open for 0% of the time, Pallas kernels for 0%

commit v1 on v0

v1 whole, which is shorter than its diff:
```python
import jax
import jax.numpy as jnp
from jax import lax
from jax.experimental import pallas as pl
from jax.experimental.pallas import tpu as pltpu
from jax.sharding import PartitionSpec as P

MESH = pl.DeviceIdType.MESH
N = 1024
R = 64
SP = 16
F32 = jnp.float32
BF = jnp.bfloat16


def dot_nt(a, b):
    return lax.dot_general(a, b, (((1,), (1,)), ((), ())), preferred_element_type=F32)


def kernel(
    dinv_ref, coupling_ref, pos_ref, pattern_ref, basis_ref,
    sigma_ref, grad_ref,
    w, x2, zbuf, dbuf, eterm, vterm, state, arrived, sent_final, got_final,
    basis, pieces_out, pieces_in, rows_out, rows_in,
    local_sem, core_send, core_recv, shift_send, shift_recv, ex_send, ex_recv, rows_send, rows_recv, swap_send, swap_recv,
):
    tm, sp = lax.axis_index("tm"), lax.axis_index("space")
    y, c = tm // 2, tm % 2
    zc, xc = sp // 4, sp % 4
    other = 1 - c
    partner = (y * 2 + other, sp)
    chain_core = jnp.where((y == 1) | (y == 2), 1, 0)
    chain = c == chain_core
    y_odd = y % 2 == 1
    last = y == 3

    load_c = pltpu.make_async_copy(coupling_ref, w.at[c], local_sem.at[0])
    load_c.start()
    load_b = pltpu.make_async_copy(basis_ref, basis, local_sem.at[1])
    load_b.start()
    dbuf[pl.ds(c, 1)] = dinv_ref[...][None]

    barrier = pltpu.get_barrier_semaphore()

    def greet(t, s):
        pl.semaphore_signal(barrier, inc=1, device_id=(t, s), device_id_type=MESH)

    for d in range(1, SP):
        greet(tm, (sp + d) % SP)
    greet(*partner)
    for dy in (1, 3):
        for core in (0, 1):
            greet(((y + dy) % 4) * 2 + core, sp)
    pl.semaphore_wait(barrier, SP + 4)

    core_d = pltpu.make_async_remote_copy(
        src_ref=dinv_ref, dst_ref=dbuf.at[c], send_sem=core_send.at[0], recv_sem=core_recv.at[0],
        device_id=partner, device_id_type=MESH)
    core_d.start()
    load_c.wait()
    core_c = pltpu.make_async_remote_copy(
        src_ref=w.at[c], dst_ref=w.at[c], send_sem=core_send.at[1], recv_sem=core_recv.at[1],
        device_id=partner, device_id_type=MESH)
    core_c.start()

    lane = lax.broadcasted_iota(jnp.int32, (1, 1, 128), 2)
    low = lane < R
    pick = low != (sp % 2 == 1)
    eye = (lax.broadcasted_iota(jnp.int32, (256, 256), 0)
           == lax.broadcasted_iota(jnp.int32, (256, 256), 1)).astype(BF)

    def set_x(value):
        x2[0:R] = value
        x2[R:2 * R] = value

    def exchange(k, chunk):
        for dz in (2, 1, 3, 0):
            q = (zc + dz) % 4
            v = chunk(q).reshape(4, 2, 32, 128)
            packed = jnp.where(pick, v[:, 0], v[:, 1])
            pieces_out[k, pl.ds(4 * q, 4)] = packed.astype(BF)
            for dx in (2, 1, 3, 0):
                i = 4 * q + (xc + dx) % 4
                if dz == 0 and dx == 0:
                    pieces_in[k, pl.ds(sp, 1)] = pieces_out[k, pl.ds(sp, 1)]
                else:
                    pltpu.make_async_remote_copy(
                        src_ref=pieces_out.at[k, i], dst_ref=pieces_in.at[k, sp],
                        send_sem=ex_send.at[k], recv_sem=ex_recv.at[k],
                        device_id=(tm, i), device_id_type=MESH).start()

    def exchange_desc(k):
        return pltpu.make_async_remote_copy(
            src_ref=pieces_out.at[k, pl.ds(0, SP - 1)], dst_ref=pieces_in.at[k, pl.ds(0, SP - 1)],
            send_sem=ex_send.at[k], recv_sem=ex_recv.at[k], device_id=partner, device_id_type=MESH)

    def product_chunk(slot):
        def chunk(q):
            return dot_nt(w[slot, pl.ds(pl.multiple_of(256 * q, 256), 256), :], x2[...])
        return chunk

    def transpose_chunk(q):
        return dot_nt(eye, x2[:, pl.ds(pl.multiple_of(256 * q, 256), 256)])

    def collect(k):
        exchange_desc(k).wait_recv()
        lo = low[0]
        for m in range(8):
            a = pieces_in[k, 2 * m].astype(F32)
            b = pieces_in[k, 2 * m + 1].astype(F32)
            zbuf[0:32, 128 * m:128 * (m + 1)] = jnp.where(lo, a, b).astype(BF)
            zbuf[32:64, 128 * m:128 * (m + 1)] = pltpu.roll(jnp.where(lo, b, a), R, 1).astype(BF)

    @pl.when(chain & y_odd)
    def _():
        core_d.wait_recv()
        set_x(dbuf[0])
        exchange(0, transpose_chunk)
        set_x(dbuf[1])

        @pl.when(c == 1)
        def _():
            core_c.wait_recv()
        exchange(1, product_chunk(0))
        collect(0)
        vterm[...] = zbuf[...].astype(F32)

    @pl.when(chain & jnp.logical_not(y_odd))
    def _():
        core_d.wait_recv()
        set_x(dbuf[1])
        exchange(0, transpose_chunk)
        vterm[...] = dbuf[0].astype(F32)
        collect(0)
        set_x(zbuf[...])

        @pl.when(c == 1)
        def _():
            core_c.wait_recv()
        exchange(1, product_chunk(0))

    @pl.when(jnp.logical_not(chain))
    def _():
        core_d.wait_recv()
        eterm[...] = dbuf[1].astype(F32)

        @pl.when(c == 1)
        def _():
            core_c.wait_recv()

        @pl.when(y == 1)
        def _():
            set_x(dbuf[1])
            exchange(0, transpose_chunk)
            collect(0)
            eterm[...] = zbuf[...].astype(F32)

    @pl.when(c == 0)
    def _():
        @pl.when(jnp.logical_not(last))
        def _():
            core_c.wait_recv()

    @pl.when(chain & jnp.logical_not(last))
    def _():
        for part in range(4):
            w[2, 256 * part:256 * (part + 1), :] = jnp.dot(
                w[0, 256 * part:256 * (part + 1), :], w[1], preferred_element_type=F32).astype(BF)

    @pl.when(chain)
    def _():
        collect(1)
        eterm[...] = vterm[...] + dot_nt(zbuf[...], w[0])

    @pl.when(last)
    def _():
        state[...] = eterm[...].astype(BF)

        @pl.when(c == 0)
        def _():
            core_c.wait_recv()

    def shift_desc(core, k):
        return pltpu.make_async_remote_copy(
            src_ref=state, dst_ref=arrived, send_sem=shift_send.at[k], recv_sem=shift_recv,
            device_id=(((y + 3) % 4) * 2 + core, sp), device_id_type=MESH)

    @pl.when(jnp.logical_not(last))
    def _():
        slot = jnp.where(chain, 2, 1)
        shift_desc(c, 0).wait_recv()
        set_x(arrived[...])
        exchange(2, product_chunk(slot))
        collect(2)
        state[...] = (eterm[...] + dot_nt(zbuf[...], w[slot])).astype(BF)

    @pl.when(chain & (y > 0))
    def _():
        next_core = jnp.where(y == 1, 0, 1)
        shift_desc(next_core, 0).start()
        shift_desc(1 - next_core, 1).start()

    convert = y_odd & jnp.logical_not(last & jnp.logical_not(chain))

    @pl.when(convert)
    def _():
        set_x(state[...])
        exchange(3, transpose_chunk)
        collect(3)
        sent_final[...] = zbuf[...]

    @pl.when(jnp.logical_not(convert))
    def _():
        sent_final[...] = state[...]

    swap = pltpu.make_async_remote_copy(
        src_ref=sent_final, dst_ref=got_final, send_sem=swap_send, recv_sem=swap_recv,
        device_id=partner, device_id_type=MESH)

    @pl.when(chain_core == 1)
    def _():
        swap.start()
        swap.wait()

    @pl.when(chain_core == 0)
    def _():
        got_final[...] = sent_final[...]

    sigma_ref[...] = got_final[...]

    position = pos_ref[...]
    target = position // R * 4 + position % 4
    slots = lax.broadcasted_iota(jnp.int32, (R, R), 0)
    place = (slots == target).astype(BF)
    ordered = jnp.dot(place, got_final[...], preferred_element_type=F32).astype(BF)
    stacked = jnp.concatenate([ordered[:, 256 * k:256 * (k + 1)] for k in range(4)], axis=0)
    ri = lax.broadcasted_iota(jnp.int32, (256, 256), 0)
    ci = lax.broadcasted_iota(jnp.int32, (256, 256), 1)
    spread = (ci == (ri % 16) // 4 * R + ri // 16 * 4 + ri % 4).astype(BF)
    rows_out[...] = jnp.dot(spread, stacked, preferred_element_type=F32).astype(BF).reshape(SP, 16, 256)
    for d in (10, 6, 14, 2, 9, 11, 5, 7, 13, 15, 1, 3, 8, 4, 12):
        i = (sp + d) % SP
        pltpu.make_async_remote_copy(
            src_ref=rows_out.at[i], dst_ref=rows_in.at[sp], send_sem=rows_send, recv_sem=rows_recv,
            device_id=(tm, i), device_id_type=MESH).start()
    rows_in[pl.ds(sp, 1)] = rows_out[pl.ds(sp, 1)]
    load_b.wait()
    rows_desc = pltpu.make_async_remote_copy(
        src_ref=rows_out.at[pl.ds(0, SP - 1)], dst_ref=rows_in.at[pl.ds(0, SP - 1)],
        send_sem=rows_send, recv_sem=rows_recv, device_id=partner, device_id_type=MESH)
    rows_desc.wait_recv()
    gather = (ci == (ri % R) // 4 * 16 + ri // R * 4 + ri % 4).astype(BF)
    mine = jnp.dot(gather, rows_in[...].reshape(256, 256), preferred_element_type=F32).astype(BF)
    block = lax.broadcasted_iota(jnp.int32, (1, 256), 1) // 128
    total = jnp.zeros((R, grad_ref.shape[1]), F32)
    for k in range(4):
        chosen = jnp.zeros((1, 256), jnp.int32)
        for n in range(pattern_ref.shape[1]):
            chosen = jnp.where(block + 2 * k == pattern_ref[0, n], 1, chosen)
        masked = jnp.where(chosen == 1, mine[R * k:R * (k + 1)].astype(F32), 0.0).astype(BF)
        total += jnp.dot(masked, basis[256 * k:256 * (k + 1), :], preferred_element_type=F32)
    grad_ref[...] = total.astype(BF)

    core_d.wait_send()
    core_c.wait_send()
    rows_desc.wait_send()

    @pl.when(chain & (y > 0))
    def _():
        shift_desc(0, 0).wait_send()
        shift_desc(0, 1).wait_send()

    @pl.when(chain | (y == 1))
    def _():
        exchange_desc(0).wait_send()

    @pl.when(chain)
    def _():
        exchange_desc(1).wait_send()

    @pl.when(jnp.logical_not(last))
    def _():
        exchange_desc(2).wait_send()

    @pl.when(convert)
    def _():
        exchange_desc(3).wait_send()


def on_device(dinv, coupling, owner_position, pattern, basis):
    vmem = pl.BlockSpec(memory_space=pltpu.VMEM)
    anywhere = pl.BlockSpec(memory_space=pl.ANY)
    smem = pl.BlockSpec(memory_space=pltpu.SMEM)
    h = basis.shape[1]
    dma = pltpu.SemaphoreType.DMA
    sigma, gradient = pl.pallas_call(
        kernel,
        out_shape=(jax.ShapeDtypeStruct((R, N), BF), jax.ShapeDtypeStruct((R, h), BF)),
        in_specs=[vmem, anywhere, vmem, smem, anywhere],
        out_specs=(vmem, vmem),
        scratch_shapes=[
            pltpu.VMEM((3, N, N), BF),
            pltpu.VMEM((2 * R, N), BF),
            pltpu.VMEM((R, N), BF),
            pltpu.VMEM((2, R, N), BF),
            pltpu.VMEM((R, N), F32),
            pltpu.VMEM((R, N), F32),
            pltpu.VMEM((R, N), BF),
            pltpu.VMEM((R, N), BF),
            pltpu.VMEM((R, N), BF),
            pltpu.VMEM((R, N), BF),
            pltpu.VMEM((N, h), BF),
            pltpu.VMEM((4, SP, 32, 128), BF),
            pltpu.VMEM((4, SP, 32, 128), BF),
            pltpu.VMEM((SP, 16, 256), BF),
            pltpu.VMEM((SP, 16, 256), BF),
            dma((2,)), dma((2,)), dma((2,)), dma((2,)), dma, dma((4,)), dma((4,)), dma, dma, dma, dma,
        ],
        compiler_params=pltpu.CompilerParams(
            collective_id=0, has_side_effects=True, vmem_limit_bytes=48 << 20),
        name="selected_inverse",
    )(dinv[0], coupling[0], owner_position[None], pattern, basis)
    return sigma[None], gradient[None]


def solution(mesh):
    placed = (P("tm", "space", None), P("tm", None, None), P("space"), P("space", None), P())
    return jax.shard_map(
        on_device,
        mesh=mesh,
        in_specs=placed,
        out_specs=(P("tm", "space", None), P("tm", "space", None)),
        check_vma=False,
    )
```

time: 490 us -> 58.1 us (0.12)
  waiting for transfers between devices: 405 us -> 0 us
  Pallas kernels: 0 us -> 50.9 us
  starting transfers between devices: 33.8 us -> 0 us
  matrix products: 28.8 us -> 0 us
  between operations: 14.1 us -> 0.65 us
    all_gather x8 -> x0, waiting for transfers between devices: 368 us -> none  [one_turn(): gathered = lax.all_gather(carried, 'space', axis=0, tiled=True)]
    pallas_call x0 -> x1, Pallas kernels: none -> 50.9 us  [on_device(): pl.pallas_call(kernel, out_shape=(jax.ShapeDtypeStruct((R, N), BF), jax.S...]
    ppermute x8 -> x0, waiting for transfers between devices: 29.8 us -> none  [shifted(): lax.ppermute(value, axis, [(source, source + steps) for source in range(l...]
    ppermute x8 -> x0, starting transfers between devices: 29.1 us -> none  [shifted(): lax.ppermute(value, axis, [(source, source + steps) for source in range(l...]
    dot_general x10 -> x0, matrix products: 28.8 us -> none  [the longest x8 26.8 us: one_turn(): lax.dot_general(product_rows, coupling[0], (((1,), (1,)), ((), ())), pref...]
    all_to_all x1 -> x0, waiting for transfers between devices: 6.72 us -> none  [on_device(): lax.all_to_all(ordered[:, 0, :], 'space', split_axis=0, concat_axis=0, ti...]
    unnamed x4 -> x12, local copies, waits for them, and re-layouts: 0.02 us -> 6.31 us
    while x32 -> x0, local copies, waits for them, and re-layouts: 5.2 us -> none
  transfers between devices with their start and end apart: 17 -> 0, of which waited for: 17 -> 0; matrix products, arithmetic and copies ran while one was open for 0% -> 0% of each run, Pallas kernels for 0% -> 0%
where the time goes in v1:
time: 58.1 us; the launch traced here: 57.9 us
  Pallas kernels  50.9 us (88%)
  local copies, waits for them, and re-layouts  6.31 us (11%)
  between operations  0.65 us (1%)
    pallas_call x1, Pallas kernels, on_device(): pl.pallas_call(kernel, out_shape=(jax.ShapeDtypeStruct((R, N), BF), jax.S...  50.9 us
    unnamed x12, local copies, waits for them, and re-layouts  6.31 us

profile of v1, /device:TPU:1, one launch (start us, length us, event | category | flops | bytes accessed | tf_op | source)
XLA Modules:
  0.0 57.9 jit_solution(12997156062973371031)
XLA Ops:
  0.6 0.0 copy-start
  0.6 1.6 %copy-done = bf16[1,1024,1024]{2,1,0:T(8,128)(2,1)S(1)} copy-done((bf16[1,1024,1024]{2,1,0:T(8,128)(2,1)S(1)}, bf16[1,1024,1024]{2,1,0:T(8,128)(2,1)}, u32[]{:S(2)}) %copy-start) | copy-done | bytes 2097176
  2.2 0.0 copy-start.1
  2.2 1.2 %copy-done.1 = bf16[1024,512]{1,0:T(8,128)(2,1)S(1)} copy-done((bf16[1024,512]{1,0:T(8,128)(2,1)S(1)}, bf16[1024,512]{1,0:T(8,128)(2,1)}, u32[]{:S(2)}) %copy-start.1) | copy-done | bytes 1048600
  3.4 0.0 copy-start.2
  3.5 0.9 %copy-done.2 = bf16[1,64,1024]{2,1,0:T(8,128)(2,1)S(1)} copy-done((bf16[1,64,1024]{2,1,0:T(8,128)(2,1)S(1)}, bf16[1,64,1024]{2,1,0:T(8,128)(2,1)}, u32[]{:S(2)}) %copy-start.2) | copy-done | bytes 131096
  4.4 0.0 copy-start.3
  4.4 0.7 %copy-done.3 = s32[64]{0:T(128)S(1)} copy-done((s32[64]{0:T(128)S(1)}, s32[64]{0:T(128)}, u32[]{:S(2)}) %copy-start.3) | copy-done | bytes 280
  5.0 0.0 copy-start.4
  5.0 0.7 %copy-done.4 = s32[1,4]{1,0:T(1,128)S(1)} copy-done((s32[1,4]{1,0:T(1,128)S(1)}, s32[1,4]{1,0:T(1,128)}, u32[]{:S(2)}) %copy-start.4) | copy-done | bytes 40
  5.7 50.9 %selected_inverse.1 = (bf16[64,1024]{1,0:T(8,128)(2,1)S(1)}, bf16[64,512]{1,0:T(8,128)(2,1)S(1)}) custom-call(bf16[64,1024]{1,0:T(8,128)(2,1)S(1)} %bitcast.6, bf16[1024,1024]{1,0:T(8,128)(2,1)S(1)} %bitcast.5, s32[1,64]{1,0:T(1,128)S(1)} %bitcast.9, s32[1,4]{1,0:T(1,128)S(1)} %copy-done.4, bf16[1024,512]{1,0:T(8,128)(2,1)S(1)} %copy-done.1), custom_call_target="tpu_custom_call" | custom-call | tf_op jit(solution)/shard_map/selected_inverse/pallas_call | solution.py:296
  56.6 0.7 %copy.9 = bf16[1,64,1024]{2,1,0:T(8,128)(2,1)} copy(bf16[1,64,1024]{2,1,0:T(8,128)(2,1)S(1)} %bitcast.7) | data formatting | bytes 262144
  57.2 0.6 %copy.10 = bf16[1,64,512]{2,1,0:T(8,128)(2,1)} copy(bf16[1,64,512]{2,1,0:T(8,128)(2,1)S(1)} %bitcast.8) | data formatting | bytes 131072
Async XLA Ops:
  0.6 1.6 %copy-start = (bf16[1,1024,1024]{2,1,0:T(8,128)(2,1)S(1)}, bf16[1,1024,1024]{2,1,0:T(8,128)(2,1)}, u32[]{:S(2)}) copy-start(bf16[1,1024,1024]{2,1,0:T(8,128)(2,1)} %param.6) | copy-start | bytes 6291460
  2.2 1.2 %copy-start.1 = (bf16[1024,512]{1,0:T(8,128)(2,1)S(1)}, bf16[1024,512]{1,0:T(8,128)(2,1)}, u32[]{:S(2)}) copy-start(bf16[1024,512]{1,0:T(8,128)(2,1)} %basis_ref.1) | copy-start | bytes 3145732
  3.4 0.9 %copy-start.2 = (bf16[1,64,1024]{2,1,0:T(8,128)(2,1)S(1)}, bf16[1,64,1024]{2,1,0:T(8,128)(2,1)}, u32[]{:S(2)}) copy-start(bf16[1,64,1024]{2,1,0:T(8,128)(2,1)} %param.5) | copy-start | bytes 393220
  4.4 0.7 %copy-start.3 = (s32[64]{0:T(128)S(1)}, s32[64]{0:T(128)}, u32[]{:S(2)}) copy-start(s32[64]{0:T(128)} %param.7) | copy-start | bytes 772
  5.0 0.7 %copy-start.4 = (s32[1,4]{1,0:T(1,128)S(1)}, s32[1,4]{1,0:T(1,128)}, u32[]{:S(2)}) copy-start(s32[1,4]{1,0:T(1,128)} %pattern_ref.1) | copy-start | bytes 52

commit v2 on v1

v2 whole, which is shorter than its diff:
```python
import jax
import jax.numpy as jnp
from jax import lax
from jax.experimental import pallas as pl
from jax.experimental.pallas import tpu as pltpu
from jax.sharding import PartitionSpec as P

MESH = pl.DeviceIdType.MESH
N = 1024
R = 64
SP = 16
F32 = jnp.float32
BF = jnp.bfloat16
FAR_FIRST = (10, 6, 14, 2, 9, 11, 5, 7, 13, 15, 1, 3, 8, 4, 12)


def dot_nt(a, b):
    return lax.dot_general(a, b, (((1,), (1,)), ((), ())), preferred_element_type=F32)


def dot_nn(a, b):
    return jnp.dot(a, b, preferred_element_type=F32)


def kernel(
    dinv_ref, coupling_ref, pos_ref, pattern_ref, basis_ref,
    sigma_ref, grad_ref,
    w, wt, wp, perm, x2, zbuf, dbuf, eterm, vterm, state, arrived, sent_final, final, basis,
    pos, pos_out, pos_in, pattern, pieces_out, pieces_in, rows_out, rows_in,
    local_sem, core_send, core_recv, shift_send, shift_recv, ex_send, ex_recv,
    rows_send, rows_recv, swap_send, swap_recv, pos_send, pos_recv,
):
    tm, sp = lax.axis_index("tm"), lax.axis_index("space")
    y, c = tm // 2, tm % 2
    zc, xc = sp // 4, sp % 4
    partner = (y * 2 + 1 - c, sp)
    chain_core = jnp.where((y == 1) | (y == 2), 1, 0)
    chain = c == chain_core
    y_odd = y % 2 == 1
    first_plane, last_plane = y == 0, y == 3
    idle = last_plane & jnp.logical_not(chain)
    no = jnp.logical_not

    load_d = pltpu.make_async_copy(dinv_ref, dbuf.at[c], local_sem.at[0])
    load_d.start()
    load_c = pltpu.make_async_copy(coupling_ref, w.at[c], local_sem.at[1])
    load_c.start()
    load_p = pltpu.make_async_copy(pos_ref, pos, local_sem.at[2])
    load_p.start()
    load_t = pltpu.make_async_copy(pattern_ref, pattern, local_sem.at[3])
    load_t.start()
    load_b = pltpu.make_async_copy(basis_ref, basis, local_sem.at[4])
    load_b.start()

    barrier = pltpu.get_barrier_semaphore()

    def greet(t, s):
        pl.semaphore_signal(barrier, inc=1, device_id=(t, s), device_id_type=MESH)

    for d in FAR_FIRST:
        greet(tm, (sp + d) % SP)
    for dy in (1, 3):
        for core in (0, 1):
            greet(((y + dy) % 4) * 2 + core, sp)
    greet(*partner)
    load_d.wait()
    load_p.wait()
    load_t.wait()
    load_c.wait()
    pl.semaphore_wait(barrier, SP + 4)

    core_d = pltpu.make_async_remote_copy(
        src_ref=dbuf.at[c], dst_ref=dbuf.at[c], send_sem=core_send.at[0], recv_sem=core_recv.at[0],
        device_id=partner, device_id_type=MESH)
    core_d.start()
    core_c = pltpu.make_async_remote_copy(
        src_ref=w.at[c], dst_ref=w.at[c], send_sem=core_send.at[1], recv_sem=core_recv.at[1],
        device_id=partner, device_id_type=MESH)
    core_c.start()

    lane = lax.broadcasted_iota(jnp.int32, (1, 1, 128), 2)
    low = lane < R
    pick = low != (sp % 2 == 1)
    ri = lax.broadcasted_iota(jnp.int32, (256, 256), 0)
    ci = lax.broadcasted_iota(jnp.int32, (256, 256), 1)
    eye = (ri == ci).astype(BF)

    def set_x(value):
        x2[0:R] = value
        x2[R:2 * R] = value

    def rows_of(ref, q):
        return ref[pl.ds(pl.multiple_of(256 * q, 256), 256), :]

    def exchange(k, *chunks):
        for dz in (2, 1, 3, 0):
            q = (zc + dz) % 4
            for h, chunk in enumerate(chunks):
                v = chunk(q).reshape(4, 2, 32, 128)
                packed = jnp.where(pick, v[:, 0], v[:, 1])
                pieces_out[k, pl.ds(4 * q, 4), h] = packed.astype(BF)
            for dx in (2, 1, 3, 0):
                i = 4 * q + (xc + dx) % 4
                if dz == 0 and dx == 0:
                    pieces_in[k, pl.ds(sp, 1)] = pieces_out[k, pl.ds(sp, 1)]
                else:
                    both = len(chunks) == 2
                    pltpu.make_async_remote_copy(
                        src_ref=pieces_out.at[k, i] if both else pieces_out.at[k, i, 0],
                        dst_ref=pieces_in.at[k, sp] if both else pieces_in.at[k, sp, 0],
                        send_sem=ex_send.at[k], recv_sem=ex_recv.at[k],
                        device_id=(tm, i), device_id_type=MESH).start()

    def exchange_desc(k, both):
        part = pl.ds(0, SP - 1)
        return pltpu.make_async_remote_copy(
            src_ref=pieces_out.at[k, part] if both else pieces_out.at[k, part, 0],
            dst_ref=pieces_in.at[k, part] if both else pieces_in.at[k, part, 0],
            send_sem=ex_send.at[k], recv_sem=ex_recv.at[k], device_id=partner, device_id_type=MESH)

    def product_chunk(slot):
        return lambda q: dot_nt(w[slot, pl.ds(pl.multiple_of(256 * q, 256), 256), :], x2[...])

    def transpose_chunk(q):
        return dot_nt(eye, x2[:, pl.ds(pl.multiple_of(256 * q, 256), 256)])

    def collect(k, both=False):
        exchange_desc(k, both).wait_recv()
        lo = low[0]
        for h in range(2 if both else 1):
            for m in range(8):
                a = pieces_in[k, 2 * m, h].astype(F32)
                b = pieces_in[k, 2 * m + 1, h].astype(F32)
                columns = slice(128 * m, 128 * (m + 1))
                zbuf[R * h:R * h + 32, columns] = jnp.where(lo, a, b).astype(BF)
                zbuf[R * h + 32:R * h + 64, columns] = pltpu.roll(jnp.where(lo, b, a), R, 1).astype(BF)

    def transpose_w(to, slot):
        for p in range(4):
            wt[to, :, 256 * p:256 * (p + 1)] = w[slot, 256 * p:256 * (p + 1), :].T

    def send_rows(value):
        position = pos[...]
        target = position // R * 4 + position % 4
        place = (lax.broadcasted_iota(jnp.int32, (R, R), 0) == target).astype(BF)
        ordered = dot_nn(place, value).astype(BF)
        stacked = jnp.concatenate([ordered[:, 256 * k:256 * (k + 1)] for k in range(4)], axis=0)
        spread = (ci == (ri % 16) // 4 * R + ri // 16 * 4 + ri % 4).astype(BF)
        rows_out[...] = dot_nn(spread, stacked).astype(BF).reshape(SP, 16, 256)
        for d in FAR_FIRST:
            i = (sp + d) % SP
            pltpu.make_async_remote_copy(
                src_ref=rows_out.at[i], dst_ref=rows_in.at[sp], send_sem=rows_send, recv_sem=rows_recv,
                device_id=(tm, i), device_id_type=MESH).start()
        rows_in[pl.ds(sp, 1)] = rows_out[pl.ds(sp, 1)]

    rows_desc = pltpu.make_async_remote_copy(
        src_ref=rows_out.at[pl.ds(0, SP - 1)], dst_ref=rows_in.at[pl.ds(0, SP - 1)],
        send_sem=rows_send, recv_sem=rows_recv, device_id=partner, device_id_type=MESH)

    def collect_rows():
        rows_desc.wait_recv()
        gather = (ci == (ri % R) // 4 * 16 + ri // R * 4 + ri % 4).astype(BF)
        return dot_nn(gather, rows_in[...].reshape(256, 256))

    @pl.when(chain & y_odd)
    def _():
        core_d.wait_recv()
        set_x(dbuf[1])

        @pl.when(c == 1)
        def _():
            core_c.wait_recv()
        exchange(1, product_chunk(0))
        set_x(dbuf[0])
        exchange(0, transpose_chunk)

    @pl.when(chain & no(y_odd))
    def _():
        core_d.wait_recv()
        set_x(dbuf[1])
        exchange(0, transpose_chunk)
        vterm[0:R] = dbuf[0].astype(F32)

    @pl.when(no(chain))
    def _():
        core_d.wait_recv()
        eterm[0:R] = dbuf[1].astype(F32)

        @pl.when(y == 1)
        def _():
            set_x(dbuf[1])
            exchange(0, transpose_chunk)

    permuted = first_plane | (y_odd & no(idle))

    def pos_desc(j, i):
        return pltpu.make_async_remote_copy(
            src_ref=pos_out, dst_ref=pos_in.at[j], send_sem=pos_send, recv_sem=pos_recv,
            device_id=(tm, i), device_id_type=MESH)

    @pl.when(permuted)
    def _():
        pos_out[...] = jnp.broadcast_to(jnp.concatenate([pos[...], pos[...]], axis=1), (8, 128))
        for d in FAR_FIRST:
            pos_desc(sp, (sp + d) % SP).start()
        pos_in[pl.ds(sp, 1)] = pos_out[...][None]

    @pl.when(first_plane | idle)
    def _():
        send_rows(dbuf[c])

    @pl.when(chain)
    def _():
        @pl.when(c == 1)
        def _():
            @pl.when(no(y_odd))
            def _():
                core_c.wait_recv()
        transpose_w(0, 0)

    pos_all = pltpu.make_async_remote_copy(
        src_ref=pos_in.at[pl.ds(0, SP - 1)], dst_ref=pos_in.at[pl.ds(0, SP - 1)],
        send_sem=pos_send, recv_sem=pos_recv, device_id=partner, device_id_type=MESH)

    @pl.when(permuted)
    def _():
        pos_all.wait_recv()
        p_index = lax.broadcasted_iota(jnp.int32, (N, 128), 0)
        for m in range(8):
            row = jnp.where(low[0], pos_in[2 * m, 0:1], pos_in[2 * m + 1, 0:1])
            perm[:, 128 * m:128 * (m + 1)] = (p_index == row).astype(BF)

    def permuted_chunk(ref):
        return lambda q: dot_nn(rows_of(perm, q), ref[...])

    @pl.when(chain & no(y_odd))
    def _():
        collect(0)
        set_x(zbuf[0:R])

        @pl.when(first_plane)
        def _():
            wp[:, 0:128] = dot_nt(w[0], x2[...]).astype(BF)
            exchange(1, lambda q: rows_of(wp, q)[:, 0:128].astype(F32), permuted_chunk(wp.at[:, 0:128]))

        @pl.when(no(first_plane))
        def _():
            exchange(1, product_chunk(0))

    @pl.when((y_odd & chain) | (no(chain) & (y == 1)))
    def _():
        collect(0)

        @pl.when(chain)
        def _():
            vterm[0:R] = zbuf[0:R].astype(F32)

        @pl.when(no(chain))
        def _():
            eterm[0:R] = zbuf[0:R].astype(F32)

    @pl.when(no(chain & (c == 1)))
    def _():
        core_c.wait_recv()

    @pl.when(chain & no(last_plane))
    def _():
        for part in range(4):
            rows = slice(256 * part, 256 * (part + 1))
            w[2, rows, :] = dot_nn(w[0, rows, :], w[1]).astype(BF)
        transpose_w(1, 2)

    @pl.when(no(chain) & no(last_plane))
    def _():
        transpose_w(1, 1)

    slot = jnp.where(chain, 2, 1)

    @pl.when(first_plane)
    def _():
        own = collect_rows()
        for k in range(4):
            columns = slice(256 * k, 256 * (k + 1))
            vterm[R:2 * R, columns] = own[R * k:R * (k + 1)]
        eterm[R:2 * R] = vterm[R:2 * R]

    @pl.when(chain)
    def _():
        @pl.when(first_plane)
        def _():
            collect(1, True)
            eterm[...] = vterm[...] + dot_nn(zbuf[...], wt[0])

        @pl.when(no(first_plane))
        def _():
            collect(1)
            eterm[0:R] = vterm[0:R] + dot_nn(zbuf[0:R], wt[0])

    @pl.when(first_plane)
    def _():
        for part in range(4):
            rows = slice(256 * part, 256 * (part + 1))
            wp[rows, :] = dot_nn(perm[rows, :], w[slot]).astype(BF)

    next_core = jnp.where(y == 1, 0, 1)

    def shift(n, core, k):
        return pltpu.make_async_remote_copy(
            src_ref=state.at[n], dst_ref=arrived.at[n], send_sem=shift_send.at[k], recv_sem=shift_recv,
            device_id=(((y + 3) % 4) * 2 + core, sp), device_id_type=MESH)

    def shift_all(k):
        return pltpu.make_async_remote_copy(
            src_ref=state, dst_ref=arrived, send_sem=shift_send.at[k], recv_sem=shift_recv,
            device_id=(((y + 3) % 4) * 2, sp), device_id_type=MESH)

    @pl.when(last_plane)
    def _():
        for n in range(4):
            state[n] = eterm[0:R, 256 * n:256 * (n + 1)].astype(BF)

            @pl.when(chain)
            def _():
                shift(n, next_core, 0).start()

    @pl.when(no(last_plane))
    def _():
        shift_all(0).wait_recv()
        for n in range(4):
            for h in range(2):
                x2[R * h:R * (h + 1), 256 * n:256 * (n + 1)] = arrived[n]

    @pl.when(no(last_plane) & no(first_plane))
    def _():
        exchange(2, product_chunk(slot))
        collect(2)
        for n in range(4):
            columns = slice(256 * n, 256 * (n + 1))
            state[n] = (eterm[0:R, columns] + dot_nn(zbuf[0:R], wt[1, :, columns])).astype(BF)

            @pl.when(chain)
            def _():
                shift(n, next_core, 0).start()

    @pl.when(chain & no(first_plane))
    def _():
        for n in range(4):
            shift(n, 1 - next_core, 1).start()

    @pl.when(first_plane)
    def _():
        exchange(2, product_chunk(slot), lambda q: dot_nt(rows_of(wp, q), x2[...]))
        collect(2, True)
        final[...] = (eterm[...] + dot_nn(zbuf[...], wt[1])).astype(BF)

    def swap(rows):
        return pltpu.make_async_remote_copy(
            src_ref=sent_final.at[pl.ds(0, rows)], dst_ref=final.at[pl.ds(0, rows)],
            send_sem=swap_send, recv_sem=swap_recv, device_id=partner, device_id_type=MESH)

    convert = y_odd & no(idle)

    @pl.when(convert)
    def _():
        for n in range(4):
            for h in range(2):
                x2[R * h:R * (h + 1), 256 * n:256 * (n + 1)] = state[n]
        exchange(3, transpose_chunk, lambda q: dot_nt(rows_of(perm, q), x2[...]))
        collect(3, True)

        @pl.when(y == 1)
        def _():
            sent_final[...] = zbuf[...]
            swap(2 * R).start()
            swap(2 * R).wait()

        @pl.when(last_plane)
        def _():
            final[...] = zbuf[...]

    @pl.when(y == 2)
    def _():
        for n in range(4):
            sent_final[0:R, 256 * n:256 * (n + 1)] = state[n]
        swap(R).start()
        swap(R).wait()
        send_rows(final[0:R])

    @pl.when(idle)
    def _():
        final[0:R] = dbuf[1]

    @pl.when(idle | (y == 2))
    def _():
        own = collect_rows().astype(BF)
        for k in range(4):
            final[R:2 * R, 256 * k:256 * (k + 1)] = own[R * k:R * (k + 1)]

    sigma_ref[...] = final[0:R]
    load_b.wait()
    block = lax.broadcasted_iota(jnp.int32, (1, N), 1) // 128
    chosen = jnp.zeros((1, N), jnp.int32)
    for n in range(pattern_ref.shape[1]):
        chosen = jnp.where(block == pattern[0, n], 1, chosen)
    masked = jnp.where(chosen == 1, final[R:2 * R].astype(F32), 0.0).astype(BF)
    grad_ref[...] = dot_nn(masked, basis[...]).astype(BF)

    core_d.wait_send()
    core_c.wait_send()

    @pl.when(first_plane | idle | (y == 2))
    def _():
        rows_desc.wait_send()

    @pl.when(permuted)
    def _():
        pos_all.wait_send()

    @pl.when(chain & no(first_plane))
    def _():
        shift_all(0).wait_send()
        shift_all(1).wait_send()

    @pl.when(chain | (y == 1))
    def _():
        exchange_desc(0, False).wait_send()

    @pl.when(chain & no(first_plane))
    def _():
        exchange_desc(1, False).wait_send()

    @pl.when(chain & first_plane)
    def _():
        exchange_desc(1, True).wait_send()

    @pl.when(first_plane)
    def _():
        exchange_desc(2, True).wait_send()

    @pl.when(no(last_plane) & no(first_plane))
    def _():
        exchange_desc(2, False).wait_send()

    @pl.when(convert)
    def _():
        exchange_desc(3, True).wait_send()


def on_device(dinv, coupling, owner_position, pattern, basis):
    vmem = pl.BlockSpec(memory_space=pltpu.VMEM)
    hbm = pl.BlockSpec(memory_space=pltpu.HBM)
    h = basis.shape[1]
    dma = pltpu.SemaphoreType.DMA
    sigma, gradient = pl.pallas_call(
        kernel,
        out_shape=(jax.ShapeDtypeStruct((R, N), BF), jax.ShapeDtypeStruct((R, h), BF)),
        in_specs=[hbm] * 5,
        out_specs=(vmem, vmem),
        scratch_shapes=[
            pltpu.VMEM((3, N, N), BF),
            pltpu.VMEM((2, N, N), BF),
            pltpu.VMEM((N, N), BF),
            pltpu.VMEM((N, N), BF),
            pltpu.VMEM((2 * R, N), BF),
            pltpu.VMEM((2 * R, N), BF),
            pltpu.VMEM((2, R, N), BF),
            pltpu.VMEM((2 * R, N), F32),
            pltpu.VMEM((2 * R, N), F32),
            pltpu.VMEM((4, R, 256), BF),
            pltpu.VMEM((4, R, 256), BF),
            pltpu.VMEM((2 * R, N), BF),
            pltpu.VMEM((2 * R, N), BF),
            pltpu.VMEM((N, h), BF),
            pltpu.VMEM((1, R), jnp.int32),
            pltpu.VMEM((8, 128), jnp.int32),
            pltpu.VMEM((SP, 8, 128), jnp.int32),
            pltpu.SMEM((1, 4), jnp.int32),
            pltpu.VMEM((4, SP, 2, 32, 128), BF),
            pltpu.VMEM((4, SP, 2, 32, 128), BF),
            pltpu.VMEM((SP, 16, 256), BF),
            pltpu.VMEM((SP, 16, 256), BF),
            dma((5,)), dma((2,)), dma((2,)), dma((2,)), dma, dma((4,)), dma((4,)), dma, dma, dma, dma, dma, dma,
        ],
        compiler_params=pltpu.CompilerParams(
            collective_id=0, has_side_effects=True, vmem_limit_bytes=48 << 20),
        name="selected_inverse",
    )(*[
        pltpu.with_memory_space_constraint(a, pltpu.HBM)
        for a in (dinv[0], coupling[0], owner_position[None], pattern, basis)
    ])
    return sigma[None], gradient[None]


def solution(mesh):
    placed = (P("tm", "space", None), P("tm", None, None), P("space"), P("space", None), P())
    return jax.shard_map(
        on_device,
        mesh=mesh,
        in_specs=placed,
        out_specs=(P("tm", "space", None), P("tm", "space", None)),
        check_vma=False,
    )
```

time: 58.1 us -> 48.5 us (0.83)
  local copies, waits for them, and re-layouts: 6.31 us -> 1.29 us
  Pallas kernels: 50.9 us -> 46.5 us
    unnamed x12 -> x2, local copies, waits for them, and re-layouts: 6.31 us -> 1.29 us
    pallas_call x1, Pallas kernels: 50.9 us -> 46.5 us  [on_device(): pl.pallas_call(kernel, out_shape=(jax.ShapeDtypeStruct((R, N), BF), jax.S...]
where the time goes in v2:
time: 48.5 us; the launch traced here: 48.4 us
  Pallas kernels  46.5 us (96%)
  local copies, waits for them, and re-layouts  1.29 us (3%)
  between operations  0.64 us (1%)
    pallas_call x1, Pallas kernels, on_device(): pl.pallas_call(kernel, out_shape=(jax.ShapeDtypeStruct((R, N), BF), jax.S...  46.5 us
    unnamed x2, local copies, waits for them, and re-layouts  1.29 us

profile of v2, /device:TPU:1, one launch (start us, length us, event | category | flops | bytes accessed | tf_op | source)
XLA Modules:
  0.0 48.4 jit_solution(1908752241825134068)
XLA Ops:
  0.6 46.5 %selected_inverse.1 = (bf16[64,1024]{1,0:T(8,128)(2,1)S(1)}, bf16[64,512]{1,0:T(8,128)(2,1)S(1)}) custom-call(bf16[64,1024]{1,0:T(8,128)(2,1)} %bitcast.8, bf16[1024,1024]{1,0:T(8,128)(2,1)} %bitcast.7, s32[1,64]{1,0:T(1,128)} %bitcast.9, s32[1,4]{1,0:T(1,128)} %pattern_ref.1, bf16[1024,512]{1,0:T(8,128)(2,1)} %basis_ref.1), custom_call_target="tpu_custom_call" | custom-call | tf_op jit(solution)/shard_map/selected_inverse/pallas_call | solution.py:455
  47.1 0.7 %copy.9 = bf16[1,64,1024]{2,1,0:T(8,128)(2,1)} copy(bf16[1,64,1024]{2,1,0:T(8,128)(2,1)S(1)} %bitcast.5) | data formatting | bytes 262144
  47.8 0.6 %copy.10 = bf16[1,64,512]{2,1,0:T(8,128)(2,1)} copy(bf16[1,64,512]{2,1,0:T(8,128)(2,1)S(1)} %bitcast.6) | data formatting | bytes 131072

commit v3 on v0

v3 whole, which is shorter than its diff:
```python
import jax
import jax.numpy as jnp
from jax import lax
from jax.experimental import pallas as pl
from jax.experimental.pallas import tpu as pltpu
from jax.sharding import PartitionSpec as P

MESH = pl.DeviceIdType.MESH
N = 1024
R = 64
SP = 16
F32 = jnp.float32
BF = jnp.bfloat16
FAR_FIRST = (10, 6, 14, 2, 9, 11, 5, 7, 13, 15, 1, 3, 8, 4, 12)


def dot_nt(a, b):
    return lax.dot_general(a, b, (((1,), (1,)), ((), ())), preferred_element_type=F32)


def dot_nn(a, b):
    return jnp.dot(a, b, preferred_element_type=F32)


def kernel(
    dinv_ref, coupling_ref, pos_ref, pattern_ref, basis_ref,
    sigma_ref, grad_ref,
    w, wt, wp, perm, x2, x3, zbuf, dbuf, eterm, vterm, state, arrived, u_out, u_in, d_in, sent_final, final, basis,
    pos, pos_out, pos_in, pattern, pieces_out, pieces_in, rows_out, rows_in,
    local_sem, core_send, core_recv, shift_send, shift_recv, u_send, u_recv, d_recv, ex_send, ex_recv,
    rows_send, rows_recv, swap_send, swap_recv, pos_send, pos_recv, part_send, part_recv, share_send, share_recv,
):
    tm, sp = lax.axis_index("tm"), lax.axis_index("space")
    y, c = tm // 2, tm % 2
    zc, xc = sp // 4, sp % 4
    partner = (y * 2 + 1 - c, sp)
    is_a = c == jnp.where(y == 2, 1, 0)
    is_b = jnp.logical_not(is_a)
    quarter = (zc % 2) * 2 + xc % 2

    def when(condition, work):
        pl.when(condition)(work)

    def loop(count, work):
        def step(index, carry):
            work(index)
            return carry
        lax.fori_loop(0, count, step, 0)

    def block(index, size=256):
        return pl.ds(pl.multiple_of(size * index, size), size)

    def remote(src, dst, send, recv, device):
        return pltpu.make_async_remote_copy(
            src_ref=src, dst_ref=dst, send_sem=send, recv_sem=recv, device_id=device, device_id_type=MESH)

    load_d = pltpu.make_async_copy(dinv_ref, dbuf.at[c], local_sem.at[0])
    load_c = pltpu.make_async_copy(coupling_ref, w.at[c], local_sem.at[1])
    load_p = pltpu.make_async_copy(pos_ref, pos, local_sem.at[2])
    load_t = pltpu.make_async_copy(pattern_ref, pattern, local_sem.at[3])
    load_b = pltpu.make_async_copy(basis_ref, basis, local_sem.at[4])
    for load in (load_c, load_d, load_p, load_t, load_b):
        load.start()

    barrier = pltpu.get_barrier_semaphore()

    def greet(t, s):
        pl.semaphore_signal(barrier, inc=1, device_id=(t, s), device_id_type=MESH)

    for d in FAR_FIRST:
        greet(tm, (sp + d) % SP)
    for dy in (2, 1, 3):
        for core in (0, 1):
            greet(((y + dy) % 4) * 2 + core, sp)
    greet(*partner)

    lane = lax.broadcasted_iota(jnp.int32, (1, 1, 128), 2)
    low = lane < R
    lo = low[0]
    pick = low != (sp % 2 == 1)
    pick2 = pick[0]
    ri = lax.broadcasted_iota(jnp.int32, (256, 256), 0)
    ci = lax.broadcasted_iota(jnp.int32, (256, 256), 1)
    eye = (ri == ci).astype(BF)

    def transpose_w(to, slot):
        loop(4, lambda p: wt.__setitem__((to, slice(None), block(p)), w[slot, block(p), :].T))

    load_c.wait()
    when((c == 0) & (y != 2), lambda: transpose_w(0, 0))
    when((c == 1) & (y < 3), lambda: transpose_w(1, 1))
    load_d.wait()
    load_p.wait()
    load_t.wait()
    pl.semaphore_wait(barrier, SP + 6)

    core_d = remote(dbuf.at[c], dbuf.at[c], core_send.at[0], core_recv.at[0], partner)
    core_c = remote(w.at[c], w.at[c], core_send.at[1], core_recv.at[1], partner)
    copy_core = remote(w.at[3], w.at[3], core_send.at[2], core_recv.at[2], partner)
    gives_d = (c == 1) | (y == 2)
    gives_c = ((c == 1) & (y < 3)) | (y == 2)

    def part(slot, k):
        rows = pl.ds(pl.multiple_of(256 * quarter + 64 * k, 64), 64)
        return remote(w.at[slot, rows], w.at[3, rows], part_send, part_recv.at[k], (((y + 3) % 4) * 2 + 1, sp))

    def parts_sent(slot):
        return remote(w.at[slot, pl.ds(0, 256)], w.at[3, pl.ds(0, 256)], part_send, part_recv.at[0], partner)

    def share(k):
        part(3, k).wait_recv()
        first = 256 * quarter + 64 * k
        xs, zs = ((xc + 1) % 4, (xc + 3) % 4), ((zc + 1) % 4, (zc + 3) % 4)
        to = [(4 * zs[0] + xs[0], 0, 16), (4 * zs[0] + xs[1], 16, 16), (4 * zs[1] + xs[0], 32, 16), (4 * zs[1] + xs[1], 48, 16),
              (4 * zc + xs[0], 0, 32), (4 * zc + xs[1], 32, 32), (4 * zs[0] + xc, 0, 32), (4 * zs[1] + xc, 32, 32)]
        for device, offset, count in to:
            rows = pl.ds(pl.multiple_of(first + offset, 16), count)
            remote(w.at[3, rows], w.at[3, rows], share_send, share_recv, (tm, device)).start()

    shared = remote(w.at[3, pl.ds(0, 768)], w.at[3, pl.ds(0, 768)], share_send, share_recv, partner)

    def set_x(ref, value):
        ref[0:R] = value
        ref[R:2 * R] = value

    def set_x_blocks(blocks):
        for n in range(4):
            for h in range(2):
                x2[R * h:R * (h + 1), 256 * n:256 * (n + 1)] = blocks[n]

    def exchange(k, make):
        def row(step):
            dz = jnp.where(step == 0, 2, jnp.where(step == 1, 1, jnp.where(step == 2, 3, 0)))
            q = (zc + dz) % 4
            make(q, pieces_out.at[k, pl.ds(4 * q, 4)])
            for dx in (2, 1, 3, 0):
                i = 4 * q + (xc + dx) % 4

                def send(i=i):
                    remote(pieces_out.at[k, i], pieces_in.at[k, sp], ex_send.at[k], ex_recv.at[k], (tm, i)).start()
                if dx:
                    send()
                else:
                    when(dz != 0, send)
        loop(4, row)
        pieces_in[k, pl.ds(sp, 1)] = pieces_out[k, pl.ds(sp, 1)]

    def exchanged(k):
        some = pl.ds(0, SP - 1)
        return remote(pieces_out.at[k, some], pieces_in.at[k, some], ex_send.at[k], ex_recv.at[k], partner)

    def packed(*chunks):
        def make(q, out):
            for h, chunk in enumerate(chunks):
                v = chunk(q).reshape(4, 2, 32, 128)
                out[:, h] = jnp.where(pick, v[:, 0], v[:, 1]).astype(BF)
        return make

    def paired(chunk):
        def make(q, out):
            out[...] = chunk(q).reshape(4, 2, 32, 128).astype(BF)
        return make

    def collect(k, pair=False):
        exchanged(k).wait_recv()

        def columns(m):
            for h in range(2):
                a = pieces_in[k, 2 * m, h].astype(F32)
                b = pieces_in[k, 2 * m + 1, h].astype(F32)
                one, two = (32 * h, R + 32 * h) if pair else (R * h, R * h + 32)
                zbuf[one:one + 32, block(m, 128)] = jnp.where(lo, a, b).astype(BF)
                zbuf[two:two + 32, block(m, 128)] = pltpu.roll(jnp.where(lo, b, a), R, 1).astype(BF)
        loop(8, columns)

    def product_chunk(slot):
        return lambda q: dot_nt(w[slot, block(q), :], x2[...])

    def transpose_chunk(q):
        return dot_nt(eye, x2[:, block(q)])

    def perm_chunk(q):
        return dot_nt(perm[block(q), :], x2[...])

    def wp_chunk(q):
        return dot_nt(wp[block(q), :], x2[...])

    def level_chunk(q):
        return jnp.where(pick2, dot_nt(w[0, block(q), :], x2[...]), dot_nt(eye, x3[:, block(q)]))

    def send_positions():
        pos_out[...] = jnp.broadcast_to(jnp.concatenate([pos[...], pos[...]], axis=1), (8, 128))
        for d in FAR_FIRST:
            remote(pos_out, pos_in.at[sp], pos_send, pos_recv, (tm, (sp + d) % SP)).start()
        pos_in[pl.ds(sp, 1)] = pos_out[...][None]

    positions = remote(pos_in.at[pl.ds(0, SP - 1)], pos_in.at[pl.ds(0, SP - 1)], pos_send, pos_recv, partner)

    def make_perm():
        positions.wait_recv()
        p_index = lax.broadcasted_iota(jnp.int32, (N, 128), 0)

        def columns(m):
            row = jnp.where(lo, pos_in[2 * m, 0:1], pos_in[2 * m + 1, 0:1])
            perm[:, block(m, 128)] = (p_index == row).astype(BF)
        loop(8, columns)

    def make_wp(slot):
        loop(4, lambda p: wp.__setitem__((block(p), slice(None)), dot_nn(perm[block(p), :], w[slot]).astype(BF)))

    def send_rows(value):
        position = pos[...]
        target = position // R * 4 + position % 4
        place = (lax.broadcasted_iota(jnp.int32, (R, R), 0) == target).astype(BF)
        ordered = dot_nn(place, value).astype(BF)
        stacked = jnp.concatenate([ordered[:, 256 * k:256 * (k + 1)] for k in range(4)], axis=0)
        spread = (ci == (ri % 16) // 4 * R + ri // 16 * 4 + ri % 4).astype(BF)
        rows_out[...] = dot_nn(spread, stacked).astype(BF).reshape(SP, 16, 256)
        for d in FAR_FIRST:
            i = (sp + d) % SP
            remote(rows_out.at[i], rows_in.at[sp], rows_send, rows_recv, (tm, i)).start()
        rows_in[pl.ds(sp, 1)] = rows_out[pl.ds(sp, 1)]

    rows_sent = remote(rows_out.at[pl.ds(0, SP - 1)], rows_in.at[pl.ds(0, SP - 1)], rows_send, rows_recv, partner)

    def collect_rows(ref):
        rows_sent.wait_recv()
        gather = (ci == (ri % R) // 4 * 16 + ri // R * 4 + ri % 4).astype(BF)
        own = dot_nn(gather, rows_in[...].reshape(256, 256))
        for k in range(4):
            ref[R:2 * R, 256 * k:256 * (k + 1)] = own[R * k:R * (k + 1)].astype(ref.dtype)

    def shift(n, k, ref, recv, device):
        return remote(state.at[n], ref.at[n], shift_send.at[k], recv, (device, sp))

    def shifted(k):
        return remote(state, arrived, shift_send.at[k], shift_recv, partner)

    u_sent = remote(u_out, u_in, u_send.at[0], u_recv, (5, sp))
    d_sent = remote(dbuf.at[0], d_in, u_send.at[1], d_recv, (5, sp))

    give_v = remote(d_in, d_in, u_send.at[1], d_recv, partner)
    when(gives_d, core_d.start)
    when(gives_c, core_c.start)

    @pl.when(is_a)
    def _():
        @pl.when(y == 3)
        def _():
            d_sent.start()
            part(0, 0).start()
            part(0, 1).start()
        core_d.wait_recv()

        @pl.when(y == 3)
        def _():
            def columns(n):
                u_out[n] = dot_nn(dbuf[1], wt[0, :, block(n)]).astype(BF)
                remote(u_out.at[n], u_in.at[n], u_send.at[0], u_recv, (5, sp)).start()
            loop(4, columns)
            part(0, 2).start()
            part(0, 3).start()
        set_x(x2, dbuf[1])
        set_x(x3, dbuf[0])

        @pl.when(y == 2)
        def _():
            share(0)
            core_c.wait_recv()
        exchange(0, paired(level_chunk))

        @pl.when(y == 2)
        def _():
            share(1)
            d_sent.wait_recv()
            u_sent.wait_recv()
            odd = sp % 2
            for n in range(4):
                x2[pl.ds(pl.multiple_of(R * odd, R), R), 256 * n:256 * (n + 1)] = u_in[n]
            x2[pl.ds(pl.multiple_of(R * (1 - odd), R), R), :] = d_in[...]
            x3[...] = x2[...]
            loop(4, lambda n: x2.__setitem__((slice(None), block(n)), dot_nn(x3[...], wt[1, :, block(n)]).astype(BF)))
            exchange(1, paired(product_chunk(0)))
            share(2)
            share(3)
            transpose_w(0, 0)
        send_positions()

        @pl.when(y < 2)
        def _():
            core_c.wait_recv()
            w[2, block(quarter), :] = dot_nn(w[0, block(quarter), :], w[1]).astype(BF)

            @pl.when(y == 1)
            def _():
                for k in range(4):
                    part(2, k).start()
        collect(0, True)

        @pl.when(y != 2)
        def _():
            loop(4, lambda n: state.__setitem__(
                n, (dot_nn(zbuf[0:R], wt[0, :, block(n)]) + zbuf[R:2 * R, block(n)].astype(F32)).astype(BF)))

            @pl.when(y == 3)
            def _():
                for n in range(4):
                    shift(n, 0, arrived, shift_recv, 4).start()

            @pl.when(y == 1)
            def _():
                for core in (0, 1):
                    for n in range(4):
                        shift(n, core, u_in, u_recv, core).start()

        @pl.when(y == 2)
        def _():
            vterm[...] = zbuf[...].astype(F32)
            collect(1, True)
            shared.wait_recv()

            def first(n):
                x2[0:R, block(n)] = (dot_nt(zbuf[0:R], w[3, block(n), :]) + zbuf[R:2 * R, block(n)].astype(F32)).astype(BF)

            def second(n):
                x2[R:2 * R, block(n)] = (dot_nn(x2[0:R], wt[1, :, block(n)]) + vterm[0:R, block(n)]).astype(BF)

            def third(n):
                state[n] = (dot_nn(x2[R:2 * R], wt[0, :, block(n)]) + vterm[R:2 * R, block(n)]).astype(BF)
                shift(n, 0, arrived, shift_recv, 1).start()
            loop(4, first)
            loop(4, second)
            loop(4, third)
            for k, device in ((1, 2), (2, 3)):
                for n in range(4):
                    shift(n, k, arrived, shift_recv, device).start()
        make_perm()
        set_x_blocks(state)
        exchange(3, packed(transpose_chunk, perm_chunk))

        @pl.when(y < 2)
        def _():
            def rest(d):
                q = (quarter + 1 + d) % 4
                w[2, block(q), :] = dot_nn(w[0, block(q), :], w[1]).astype(BF)
            loop(3, rest)
            transpose_w(1, 2)
            make_wp(2)
        collect(3)

        @pl.when(y < 2)
        def _():
            eterm[...] = zbuf[...].astype(F32)

        @pl.when(y == 2)
        def _():
            sent_final[...] = zbuf[...]

        @pl.when(y == 3)
        def _():
            final[...] = zbuf[...]

    @pl.when(is_b & (y < 3))
    def _():
        send_positions()

        @pl.when(y == 2)
        def _():
            core_d.wait_recv()
        send_rows(dbuf[1])
        eterm[0:R] = dbuf[1].astype(F32)

        @pl.when(y == 2)
        def _():
            core_c.wait_recv()
            transpose_w(1, 1)
        make_perm()
        make_wp(1)
        collect_rows(eterm)

        @pl.when(y == 0)
        def _():
            for k in range(4):
                share(k)

    @pl.when(is_b & (y == 3))
    def _():
        send_rows(dbuf[1])
        final[0:R] = dbuf[1]
        collect_rows(final)

    slot = jnp.where(is_a, 2, 1)
    ends = (y < 2) | (is_b & (y == 2))

    @pl.when(y == 0)
    def _():
        u_sent.wait_recv()
        set_x_blocks(u_in)
        exchange(1, packed(product_chunk(slot), wp_chunk))

        @pl.when(is_b)
        def _():
            shared.wait_recv()
            copy_core.start()
            transpose_w(2, 3)

    @pl.when(ends)
    def _():
        @pl.when((y > 0) | is_b)
        def _():
            shifted(0).wait_recv()

        @pl.when((y == 0) & is_b)
        def _():
            for n in range(4):
                x3[0:R, 256 * n:256 * (n + 1)] = arrived[n]
            loop(4, lambda n: d_in.__setitem__((slice(None), block(n)), dot_nn(x3[0:R], wt[2, :, block(n)]).astype(BF)))
            give_v.start()
            set_x(x2, d_in[...])

        @pl.when((y == 0) & is_a)
        def _():
            give_v.wait_recv()
            set_x(x2, d_in[...])

        @pl.when(y > 0)
        def _():
            set_x_blocks(arrived)
        exchange(2, packed(product_chunk(slot), wp_chunk))

        @pl.when(y == 0)
        def _():
            @pl.when(is_a)
            def _():
                copy_core.wait_recv()
                transpose_w(2, 3)
            collect(1)
            vterm[...] = zbuf[...].astype(F32)
        collect(2)

        @pl.when(y == 0)
        def _():
            loop(4, lambda n: x3.__setitem__(
                (slice(None), block(n)), (dot_nn(zbuf[...], wt[2, :, block(n)]) + vterm[:, block(n)]).astype(BF)))
            zbuf[...] = x3[...]
        out = (eterm[...] + dot_nn(zbuf[...], wt[1])).astype(BF)

        @pl.when(y < 2)
        def _():
            final[...] = out

        @pl.when(y == 2)
        def _():
            sent_final[...] = out

    @pl.when(y == 2)
    def _():
        swap = remote(sent_final, final, swap_send, swap_recv, partner)
        swap.start()
        swap.wait()

    sigma_ref[...] = final[0:R]
    load_b.wait()
    column = lax.broadcasted_iota(jnp.int32, (1, N), 1) // 128
    chosen = jnp.zeros((1, N), jnp.int32)
    for n in range(pattern_ref.shape[1]):
        chosen = jnp.where(column == pattern[0, n], 1, chosen)
    masked = jnp.where(chosen == 1, final[R:2 * R].astype(F32), 0.0).astype(BF)
    grad_ref[...] = dot_nn(masked, basis[...]).astype(BF)

    when(gives_d, core_d.wait_send)
    when(gives_c, core_c.wait_send)
    when((y == 0) & is_b, copy_core.wait_send)
    when(is_b, rows_sent.wait_send)
    when(is_a | (y < 3), positions.wait_send)
    when(is_a, exchanged(0).wait_send)
    when((is_a & (y == 2)) | (y == 0), exchanged(1).wait_send)
    when(ends, exchanged(2).wait_send)
    when(is_a, exchanged(3).wait_send)
    when(is_a & (y > 0), shifted(0).wait_send)
    when(is_a & ((y == 1) | (y == 2)), shifted(1).wait_send)
    when(is_a & (y == 2), shifted(2).wait_send)
    when(is_b & (y == 0), give_v.wait_send)
    when(is_a & (y == 3), u_sent.wait_send)
    when(is_a & (y == 3), d_sent.wait_send)
    when(is_a & ((y == 3) | (y == 1)), parts_sent(0).wait_send)
    when((is_a & (y == 2)) | (is_b & (y == 0)), shared.wait_send)


def on_device(dinv, coupling, owner_position, pattern, basis):
    vmem = pl.BlockSpec(memory_space=pltpu.VMEM)
    hbm = pl.BlockSpec(memory_space=pltpu.HBM)
    h = basis.shape[1]
    dma = pltpu.SemaphoreType.DMA
    operands = (dinv[0], coupling[0], owner_position[None], pattern, basis)
    sigma, gradient = pl.pallas_call(
        kernel,
        out_shape=(jax.ShapeDtypeStruct((R, N), BF), jax.ShapeDtypeStruct((R, h), BF)),
        in_specs=[hbm] * len(operands),
        out_specs=(vmem, vmem),
        scratch_shapes=[
            pltpu.VMEM((4, N, N), BF),
            pltpu.VMEM((3, N, N), BF),
            pltpu.VMEM((N, N), BF),
            pltpu.VMEM((N, N), BF),
            pltpu.VMEM((2 * R, N), BF),
            pltpu.VMEM((2 * R, N), BF),
            pltpu.VMEM((2 * R, N), BF),
            pltpu.VMEM((2, R, N), BF),
            pltpu.VMEM((2 * R, N), F32),
            pltpu.VMEM((2 * R, N), F32),
            pltpu.VMEM((4, R, 256), BF),
            pltpu.VMEM((4, R, 256), BF),
            pltpu.VMEM((4, R, 256), BF),
            pltpu.VMEM((4, R, 256), BF),
            pltpu.VMEM((R, N), BF),
            pltpu.VMEM((2 * R, N), BF),
            pltpu.VMEM((2 * R, N), BF),
            pltpu.VMEM((N, h), BF),
            pltpu.VMEM((1, R), jnp.int32),
            pltpu.VMEM((8, 128), jnp.int32),
            pltpu.VMEM((SP, 8, 128), jnp.int32),
            pltpu.SMEM((1, 4), jnp.int32),
            pltpu.VMEM((4, SP, 2, 32, 128), BF),
            pltpu.VMEM((4, SP, 2, 32, 128), BF),
            pltpu.VMEM((SP, 16, 256), BF),
            pltpu.VMEM((SP, 16, 256), BF),
            dma((5,)), dma((3,)), dma((3,)), dma((4,)), dma, dma((2,)), dma, dma, dma((4,)), dma((4,)),
            dma, dma, dma, dma, dma, dma, dma, dma((4,)), dma, dma,
        ],
        compiler_params=pltpu.CompilerParams(
            collective_id=0, has_side_effects=True, vmem_limit_bytes=48 << 20),
        name="selected_inverse",
    )(*[pltpu.with_memory_space_constraint(a, pltpu.HBM) for a in operands])
    return sigma[None], gradient[None]


def solution(mesh):
    placed = (P("tm", "space", None), P("tm", None, None), P("space"), P("space", None), P())
    return jax.shard_map(
        on_device,
        mesh=mesh,
        in_specs=placed,
        out_specs=(P("tm", "space", None), P("tm", "space", None)),
        check_vma=False,
    )
```

time: 490 us -> 43.1 us (0.09)
  waiting for transfers between devices: 405 us -> 0 us
  Pallas kernels: 0 us -> 40.4 us
  starting transfers between devices: 33.8 us -> 0 us
  matrix products: 28.8 us -> 0 us
  between operations: 14.1 us -> 0.64 us
  local copies, waits for them, and re-layouts: 6.89 us -> 1.29 us
    all_gather x8 -> x0, waiting for transfers between devices: 368 us -> none  [one_turn(): gathered = lax.all_gather(carried, 'space', axis=0, tiled=True)]
    pallas_call x0 -> x1, Pallas kernels: none -> 40.4 us  [on_device(): pl.pallas_call(kernel, out_shape=(jax.ShapeDtypeStruct((R, N), BF), jax.S...]
    ppermute x8 -> x0, waiting for transfers between devices: 29.8 us -> none  [shifted(): lax.ppermute(value, axis, [(source, source + steps) for source in range(l...]
    ppermute x8 -> x0, starting transfers between devices: 29.1 us -> none  [shifted(): lax.ppermute(value, axis, [(source, source + steps) for source in range(l...]
    dot_general x10 -> x0, matrix products: 28.8 us -> none  [the longest x8 26.8 us: one_turn(): lax.dot_general(product_rows, coupling[0], (((1,), (1,)), ((), ())), pref...]
    all_to_all x1 -> x0, waiting for transfers between devices: 6.72 us -> none  [on_device(): lax.all_to_all(ordered[:, 0, :], 'space', split_axis=0, concat_axis=0, ti...]
    while x32 -> x0, local copies, waits for them, and re-layouts: 5.2 us -> none
  transfers between devices with their start and end apart: 17 -> 0, of which waited for: 17 -> 0; matrix products, arithmetic and copies ran while one was open for 0% -> 0% of each run, Pallas kernels for 0% -> 0%
where the time goes in v3:
time: 43.1 us; the launch traced here: 42.4 us
  Pallas kernels  40.4 us (94%)
  local copies, waits for them, and re-layouts  1.29 us (3%)
  between operations  0.64 us (1%)
    pallas_call x1, Pallas kernels, on_device(): pl.pallas_call(kernel, out_shape=(jax.ShapeDtypeStruct((R, N), BF), jax.S...  40.4 us
    unnamed x2, local copies, waits for them, and re-layouts  1.29 us

profile of v3, /device:TPU:1, one launch (start us, length us, event | category | flops | bytes accessed | tf_op | source)
XLA Modules:
  0.0 42.4 jit_solution(5771073704192573417)
XLA Ops:
  0.6 40.4 %selected_inverse.1 = (bf16[64,1024]{1,0:T(8,128)(2,1)S(1)}, bf16[64,512]{1,0:T(8,128)(2,1)S(1)}) custom-call(bf16[64,1024]{1,0:T(8,128)(2,1)} %bitcast.8, bf16[1024,1024]{1,0:T(8,128)(2,1)} %bitcast.7, s32[1,64]{1,0:T(1,128)} %bitcast.9, s32[1,4]{1,0:T(1,128)} %pattern_ref.1, bf16[1024,512]{1,0:T(8,128)(2,1)} %basis_ref.1), custom_call_target="tpu_custom_call" | custom-call | tf_op jit(solution)/shard_map/selected_inverse/pallas_call | solution.py:496
  41.1 0.7 %copy.9 = bf16[1,64,1024]{2,1,0:T(8,128)(2,1)} copy(bf16[1,64,1024]{2,1,0:T(8,128)(2,1)S(1)} %bitcast.5) | data formatting | bytes 262144
  41.7 0.6 %copy.10 = bf16[1,64,512]{2,1,0:T(8,128)(2,1)} copy(bf16[1,64,512]{2,1,0:T(8,128)(2,1)S(1)} %bitcast.6) | data formatting | bytes 131072

commit v4 on v3

--- a/solution.py
+++ b/solution.py
@@ -42,12 +42,12 @@
         pl.when(condition)(work)
 
     def loop(count, work):
-        def step(index, carry):
+        for index in range(count):
             work(index)
-            return carry
-        lax.fori_loop(0, count, step, 0)
 
     def block(index, size=256):
+        if isinstance(index, int):
+            return slice(size * index, size * (index + 1))
         return pl.ds(pl.multiple_of(size * index, size), size)
 
     def remote(src, dst, send, recv, device):
@@ -73,6 +73,13 @@
         for core in (0, 1):
             greet(((y + dy) % 4) * 2 + core, sp)
     greet(*partner)
+
+    crossing = (tm == 5) | (tm == 7)
+
+    @pl.when(crossing)
+    def _():
+        for d in FAR_FIRST:
+            greet(12 - tm, (sp + d) % SP)
 
     lane = lax.broadcasted_iota(jnp.int32, (1, 1, 128), 2)
     low = lane < R
@@ -92,13 +99,13 @@
     load_d.wait()
     load_p.wait()
     load_t.wait()
-    pl.semaphore_wait(barrier, SP + 6)
+    pl.semaphore_wait(barrier, SP + 6 + jnp.where(crossing, SP - 1, 0))
 
     core_d = remote(dbuf.at[c], dbuf.at[c], core_send.at[0], core_recv.at[0], partner)
     core_c = remote(w.at[c], w.at[c], core_send.at[1], core_recv.at[1], partner)
     copy_core = remote(w.at[3], w.at[3], core_send.at[2], core_recv.at[2], partner)
     gives_d = (c == 1) | (y == 2)
-    gives_c = ((c == 1) & (y < 3)) | (y == 2)
+    gives_c = ((c == 1) & (y < 3)) | ((c == 0) & (y > 1))
 
     def part(slot, k):
         rows = pl.ds(pl.multiple_of(256 * quarter + 64 * k, 64), 64)
@@ -128,25 +135,20 @@
             for h in range(2):
                 x2[R * h:R * (h + 1), 256 * n:256 * (n + 1)] = blocks[n]
 
-    def exchange(k, make):
-        def row(step):
-            dz = jnp.where(step == 0, 2, jnp.where(step == 1, 1, jnp.where(step == 2, 3, 0)))
+    def exchange(k, make, to=None):
+        for dz in (2, 1, 3, 0):
             q = (zc + dz) % 4
             make(q, pieces_out.at[k, pl.ds(4 * q, 4)])
             for dx in (2, 1, 3, 0):
                 i = 4 * q + (xc + dx) % 4
-
-                def send(i=i):
-                    remote(pieces_out.at[k, i], pieces_in.at[k, sp], ex_send.at[k], ex_recv.at[k], (tm, i)).start()
-                if dx:
-                    send()
-                else:
-                    when(dz != 0, send)
-        loop(4, row)
-        pieces_in[k, pl.ds(sp, 1)] = pieces_out[k, pl.ds(sp, 1)]
-
-    def exchanged(k):
-        some = pl.ds(0, SP - 1)
+                if dz or dx or to is not None:
+                    remote(pieces_out.at[k, i], pieces_in.at[k, sp], ex_send.at[k], ex_recv.at[k],
+                           (tm if to is None else to, i)).start()
+        if to is None:
+            pieces_in[k, pl.ds(sp, 1)] = pieces_out[k, pl.ds(sp, 1)]
+
+    def exchanged(k, count=SP - 1):
+        some = pl.ds(0, count)
         return remote(pieces_out.at[k, some], pieces_in.at[k, some], ex_send.at[k], ex_recv.at[k], partner)
 
     def packed(*chunks):
@@ -161,8 +163,8 @@
             out[...] = chunk(q).reshape(4, 2, 32, 128).astype(BF)
         return make
 
-    def collect(k, pair=False):
-        exchanged(k).wait_recv()
+    def collect(k, pair=False, count=SP - 1):
+        exchanged(k, count).wait_recv()
 
         def columns(m):
             for h in range(2):
@@ -239,6 +241,7 @@
     u_sent = remote(u_out, u_in, u_send.at[0], u_recv, (5, sp))
     d_sent = remote(dbuf.at[0], d_in, u_send.at[1], d_recv, (5, sp))
 
+    give_u = remote(u_in, u_in, u_send.at[0], u_recv, partner)
     give_v = remote(d_in, d_in, u_send.at[1], d_recv, partner)
     when(gives_d, core_d.start)
     when(gives_c, core_c.start)
@@ -248,8 +251,6 @@
         @pl.when(y == 3)
         def _():
             d_sent.start()
-            part(0, 0).start()
-            part(0, 1).start()
         core_d.wait_recv()
 
         @pl.when(y == 3)
@@ -258,33 +259,23 @@
                 u_out[n] = dot_nn(dbuf[1], wt[0, :, block(n)]).astype(BF)
                 remote(u_out.at[n], u_in.at[n], u_send.at[0], u_recv, (5, sp)).start()
             loop(4, columns)
-            part(0, 2).start()
-            part(0, 3).start()
-        set_x(x2, dbuf[1])
-        set_x(x3, dbuf[0])
 
         @pl.when(y == 2)
         def _():
-            share(0)
-            core_c.wait_recv()
-        exchange(0, paired(level_chunk))
-
-        @pl.when(y == 2)
-        def _():
-            share(1)
             d_sent.wait_recv()
             u_sent.wait_recv()
             odd = sp % 2
             for n in range(4):
                 x2[pl.ds(pl.multiple_of(R * odd, R), R), 256 * n:256 * (n + 1)] = u_in[n]
             x2[pl.ds(pl.multiple_of(R * (1 - odd), R), R), :] = d_in[...]
-            x3[...] = x2[...]
-            loop(4, lambda n: x2.__setitem__((slice(None), block(n)), dot_nn(x3[...], wt[1, :, block(n)]).astype(BF)))
-            exchange(1, paired(product_chunk(0)))
-            share(2)
-            share(3)
-            transpose_w(0, 0)
+            x2[...] = dot_nn(x2[...], wt[1]).astype(BF)
+            core_c.wait_recv()
+            exchange(1, paired(product_chunk(0)), 7)
+        set_x(x2, dbuf[1])
+        set_x(x3, dbuf[0])
+        exchange(0, paired(level_chunk))
         send_positions()
+        when(y == 2, lambda: transpose_w(0, 0))
 
         @pl.when(y < 2)
         def _():
@@ -299,8 +290,9 @@
 
         @pl.when(y != 2)
         def _():
-            loop(4, lambda n: state.__setitem__(
-                n, (dot_nn(zbuf[0:R], wt[0, :, block(n)]) + zbuf[R:2 * R, block(n)].astype(F32)).astype(BF)))
+            e = (dot_nn(zbuf[0:R], wt[0]) + zbuf[R:2 * R].astype(F32)).astype(BF)
+            for n in range(4):
+                state[n] = e[:, 256 * n:256 * (n + 1)]
 
             @pl.when(y == 3)
             def _():
@@ -309,32 +301,26 @@
 
             @pl.when(y == 1)
             def _():
-                for core in (0, 1):
-                    for n in range(4):
-                        shift(n, core, u_in, u_recv, core).start()
+                for n in range(4):
+                    shift(n, 0, u_in, u_recv, 1).start()
 
         @pl.when(y == 2)
         def _():
             vterm[...] = zbuf[...].astype(F32)
-            collect(1, True)
-            shared.wait_recv()
-
-            def first(n):
-                x2[0:R, block(n)] = (dot_nt(zbuf[0:R], w[3, block(n), :]) + zbuf[R:2 * R, block(n)].astype(F32)).astype(BF)
-
-            def second(n):
-                x2[R:2 * R, block(n)] = (dot_nn(x2[0:R], wt[1, :, block(n)]) + vterm[0:R, block(n)]).astype(BF)
+            make_perm()
+            shifted(0).wait_recv()
+            for n in range(4):
+                x2[0:R, 256 * n:256 * (n + 1)] = arrived[n]
+            x2[R:2 * R] = (dot_nn(x2[0:R], wt[1]) + vterm[0:R]).astype(BF)
 
             def third(n):
                 state[n] = (dot_nn(x2[R:2 * R], wt[0, :, block(n)]) + vterm[R:2 * R, block(n)]).astype(BF)
                 shift(n, 0, arrived, shift_recv, 1).start()
-            loop(4, first)
-            loop(4, second)
             loop(4, third)
             for k, device in ((1, 2), (2, 3)):
                 for n in range(4):
                     shift(n, k, arrived, shift_recv, device).start()
-        make_perm()
+        when(y != 2, make_perm)
         set_x_blocks(state)
         exchange(3, packed(transpose_chunk, perm_chunk))
 
@@ -386,15 +372,29 @@
     @pl.when(is_b & (y == 3))
     def _():
         send_rows(dbuf[1])
+        core_c.wait_recv()
+        transpose_w(0, 0)
         final[0:R] = dbuf[1]
         collect_rows(final)
+        collect(1, True, SP)
+        t = (dot_nn(zbuf[0:R], wt[0]) + zbuf[R:2 * R].astype(F32)).astype(BF)
+        for n in range(4):
+            state[n] = t[:, 256 * n:256 * (n + 1)]
+            shift(n, 0, arrived, shift_recv, 5).start()
 
     slot = jnp.where(is_a, 2, 1)
     ends = (y < 2) | (is_b & (y == 2))
 
     @pl.when(y == 0)
     def _():
-        u_sent.wait_recv()
+        @pl.when(is_b)
+        def _():
+            u_sent.wait_recv()
+            give_u.start()
+
+        @pl.when(is_a)
+        def _():
+            give_u.wait_recv()
         set_x_blocks(u_in)
         exchange(1, packed(product_chunk(slot), wp_chunk))
 
@@ -414,7 +414,7 @@
         def _():
             for n in range(4):
                 x3[0:R, 256 * n:256 * (n + 1)] = arrived[n]
-            loop(4, lambda n: d_in.__setitem__((slice(None), block(n)), dot_nn(x3[0:R], wt[2, :, block(n)]).astype(BF)))
+            d_in[...] = dot_nn(x3[0:R], wt[2]).astype(BF)
             give_v.start()
             set_x(x2, d_in[...])
 
@@ -440,9 +440,7 @@
 
         @pl.when(y == 0)
         def _():
-            loop(4, lambda n: x3.__setitem__(
-                (slice(None), block(n)), (dot_nn(zbuf[...], wt[2, :, block(n)]) + vterm[:, block(n)]).astype(BF)))
-            zbuf[...] = x3[...]
+            zbuf[...] = (dot_nn(zbuf[...], wt[2]) + vterm[...]).astype(BF)
         out = (eterm[...] + dot_nn(zbuf[...], wt[1])).astype(BF)
 
         @pl.when(y < 2)
@@ -474,17 +472,19 @@
     when(is_b, rows_sent.wait_send)
     when(is_a | (y < 3), positions.wait_send)
     when(is_a, exchanged(0).wait_send)
-    when((is_a & (y == 2)) | (y == 0), exchanged(1).wait_send)
+    when(y == 0, exchanged(1).wait_send)
+    when(is_a & (y == 2), exchanged(1, SP).wait_send)
     when(ends, exchanged(2).wait_send)
     when(is_a, exchanged(3).wait_send)
-    when(is_a & (y > 0), shifted(0).wait_send)
-    when(is_a & ((y == 1) | (y == 2)), shifted(1).wait_send)
+    when((is_a & (y > 0)) | (is_b & (y == 3)), shifted(0).wait_send)
+    when(is_a & (y == 2), shifted(1).wait_send)
     when(is_a & (y == 2), shifted(2).wait_send)
     when(is_b & (y == 0), give_v.wait_send)
+    when(is_b & (y == 0), give_u.wait_send)
     when(is_a & (y == 3), u_sent.wait_send)
     when(is_a & (y == 3), d_sent.wait_send)
-    when(is_a & ((y == 3) | (y == 1)), parts_sent(0).wait_send)
-    when((is_a & (y == 2)) | (is_b & (y == 0)), shared.wait_send)
+    when(is_a & (y == 1), parts_sent(0).wait_send)
+    when(is_b & (y == 0), shared.wait_send)
 
 
 def on_device(dinv, coupling, owner_position, pattern, basis):

time: 43.1 us -> 39.1 us (0.907)
  Pallas kernels: 40.4 us -> 36.5 us
    pallas_call x1, Pallas kernels: 40.4 us -> 36.5 us  [on_device(): pl.pallas_call(kernel, out_shape=(jax.ShapeDtypeStruct((R, N), BF), jax.S...]
where the time goes in v4:
time: 39.1 us; the launch traced here: 38.4 us
  Pallas kernels  36.5 us (93%)
  local copies, waits for them, and re-layouts  1.29 us (3%)
  between operations  0.64 us (2%)
    pallas_call x1, Pallas kernels, on_device(): pl.pallas_call(kernel, out_shape=(jax.ShapeDtypeStruct((R, N), BF), jax.S...  36.5 us
    unnamed x2, local copies, waits for them, and re-layouts  1.29 us

profile of v4, /device:TPU:1, one launch (start us, length us, event | category | flops | bytes accessed | tf_op | source)
XLA Modules:
  0.0 38.4 jit_solution(6045929602942177844)
XLA Ops:
  0.6 36.5 %selected_inverse.1 = (bf16[64,1024]{1,0:T(8,128)(2,1)S(1)}, bf16[64,512]{1,0:T(8,128)(2,1)S(1)}) custom-call(bf16[64,1024]{1,0:T(8,128)(2,1)} %bitcast.8, bf16[1024,1024]{1,0:T(8,128)(2,1)} %bitcast.7, s32[1,64]{1,0:T(1,128)} %bitcast.9, s32[1,4]{1,0:T(1,128)} %pattern_ref.1, bf16[1024,512]{1,0:T(8,128)(2,1)} %basis_ref.1), custom_call_target="tpu_custom_call" | custom-call | tf_op jit(solution)/shard_map/selected_inverse/pallas_call | solution.py:496
  37.1 0.7 %copy.9 = bf16[1,64,1024]{2,1,0:T(8,128)(2,1)} copy(bf16[1,64,1024]{2,1,0:T(8,128)(2,1)S(1)} %bitcast.5) | data formatting | bytes 262144
  37.8 0.6 %copy.10 = bf16[1,64,512]{2,1,0:T(8,128)(2,1)} copy(bf16[1,64,512]{2,1,0:T(8,128)(2,1)S(1)} %bitcast.6) | data formatting | bytes 131072

commit v5 on v4

--- a/solution.py
+++ b/solution.py
@@ -28,7 +28,7 @@
     w, wt, wp, perm, x2, x3, zbuf, dbuf, eterm, vterm, state, arrived, u_out, u_in, d_in, sent_final, final, basis,
     pos, pos_out, pos_in, pattern, pieces_out, pieces_in, rows_out, rows_in,
     local_sem, core_send, core_recv, shift_send, shift_recv, u_send, u_recv, d_recv, ex_send, ex_recv,
-    rows_send, rows_recv, swap_send, swap_recv, pos_send, pos_recv, part_send, part_recv, share_send, share_recv,
+    rows_send, rows_recv, swap_send, swap_recv, pos_send, pos_recv, part_send, part_recv, share_send, share_recv, part_in,
 ):
     tm, sp = lax.axis_index("tm"), lax.axis_index("space")
     y, c = tm // 2, tm % 2
@@ -74,12 +74,11 @@
             greet(((y + dy) % 4) * 2 + core, sp)
     greet(*partner)
 
-    crossing = (tm == 5) | (tm == 7)
-
-    @pl.when(crossing)
-    def _():
-        for d in FAR_FIRST:
-            greet(12 - tm, (sp + d) % SP)
+    for left, right in ((4, 5), (5, 7)):
+        @pl.when((tm == left) | (tm == right))
+        def _():
+            for d in FAR_FIRST:
+                greet(left + right - tm, (sp + d) % SP)
 
     lane = lax.broadcasted_iota(jnp.int32, (1, 1, 128), 2)
     low = lane < R
@@ -99,11 +98,22 @@
     load_d.wait()
     load_p.wait()
     load_t.wait()
-    pl.semaphore_wait(barrier, SP + 6 + jnp.where(crossing, SP - 1, 0))
+    crossings = jnp.where(tm == 5, 2, jnp.where((tm == 4) | (tm == 7), 1, 0))
+    pl.semaphore_wait(barrier, SP + 6 + (SP - 1) * crossings)
 
     core_d = remote(dbuf.at[c], dbuf.at[c], core_send.at[0], core_recv.at[0], partner)
     core_c = remote(w.at[c], w.at[c], core_send.at[1], core_recv.at[1], partner)
+
+    def core_part(turn):
+        rows = block((zc + (2, 1, 3, 0)[turn]) % 4)
+        return remote(w.at[c, rows], w.at[c, rows], core_send.at[1], part_in.at[turn], partner)
+
+    def core_c_here():
+        for turn in range(4):
+            core_part(turn).wait_recv()
+
     copy_core = remote(w.at[3], w.at[3], core_send.at[2], core_recv.at[2], partner)
+    core_q = remote(w.at[0, block(quarter)], w.at[0, block(quarter)], core_send.at[2], core_recv.at[2], partner)
     gives_d = (c == 1) | (y == 2)
     gives_c = ((c == 1) & (y < 3)) | ((c == 0) & (y > 1))
 
@@ -135,21 +145,25 @@
             for h in range(2):
                 x2[R * h:R * (h + 1), 256 * n:256 * (n + 1)] = blocks[n]
 
-    def exchange(k, make, to=None):
+    def piece(ref, k, i, single):
+        return ref.at[k, i, 0] if single else ref.at[k, i]
+
+    def exchange(k, make, to=None, single=False, into=None):
         for dz in (2, 1, 3, 0):
             q = (zc + dz) % 4
             make(q, pieces_out.at[k, pl.ds(4 * q, 4)])
             for dx in (2, 1, 3, 0):
                 i = 4 * q + (xc + dx) % 4
                 if dz or dx or to is not None:
-                    remote(pieces_out.at[k, i], pieces_in.at[k, sp], ex_send.at[k], ex_recv.at[k],
+                    slot = k if into is None else into
+                    remote(piece(pieces_out, k, i, single), piece(pieces_in, slot, sp, single), ex_send.at[k], ex_recv.at[slot],
                            (tm if to is None else to, i)).start()
         if to is None:
             pieces_in[k, pl.ds(sp, 1)] = pieces_out[k, pl.ds(sp, 1)]
 
-    def exchanged(k, count=SP - 1):
+    def exchanged(k, count=SP - 1, single=False):
         some = pl.ds(0, count)
-        return remote(pieces_out.at[k, some], pieces_in.at[k, some], ex_send.at[k], ex_recv.at[k], partner)
+        return remote(piece(pieces_out, k, some, single), piece(pieces_in, k, some, single), ex_send.at[k], ex_recv.at[k], partner)
 
     def packed(*chunks):
         def make(q, out):
@@ -163,11 +177,11 @@
             out[...] = chunk(q).reshape(4, 2, 32, 128).astype(BF)
         return make
 
-    def collect(k, pair=False, count=SP - 1):
-        exchanged(k, count).wait_recv()
+    def collect(k, pair=False, count=SP - 1, single=False):
+        exchanged(k, count, single).wait_recv()
 
         def columns(m):
-            for h in range(2):
+            for h in range(1 if single else 2):
                 a = pieces_in[k, 2 * m, h].astype(F32)
                 b = pieces_in[k, 2 * m + 1, h].astype(F32)
                 one, two = (32 * h, R + 32 * h) if pair else (R * h, R * h + 32)
@@ -233,63 +247,69 @@
             ref[R:2 * R, 256 * k:256 * (k + 1)] = own[R * k:R * (k + 1)].astype(ref.dtype)
 
     def shift(n, k, ref, recv, device):
-        return remote(state.at[n], ref.at[n], shift_send.at[k], recv, (device, sp))
+        return remote(state.at[n], ref.at[n], shift_send.at[k], recv.at[n], (device, sp))
 
     def shifted(k):
-        return remote(state, arrived, shift_send.at[k], shift_recv, partner)
-
-    u_sent = remote(u_out, u_in, u_send.at[0], u_recv, (5, sp))
-    d_sent = remote(dbuf.at[0], d_in, u_send.at[1], d_recv, (5, sp))
-
-    give_u = remote(u_in, u_in, u_send.at[0], u_recv, partner)
+        return remote(state, arrived, shift_send.at[k], shift_recv.at[0], partner)
+
+    def arrive(n):
+        remote(state.at[n], arrived.at[n], shift_send.at[0], shift_recv.at[n], partner).wait_recv()
+
+    def u_arrive(n):
+        remote(u_out.at[n], u_in.at[n], u_send.at[0], u_recv.at[n], partner).wait_recv()
+
+    u_sent = remote(u_out, u_in, u_send.at[0], u_recv.at[0], (5, sp))
+    d_sent = remote(dbuf.at[0], d_in, u_send.at[1], d_recv, (4, sp))
+
+    give_u = remote(u_in, u_in, u_send.at[0], u_recv.at[0], partner)
     give_v = remote(d_in, d_in, u_send.at[1], d_recv, partner)
+    when(is_a & (y == 1), core_q.start)
     when(gives_d, core_d.start)
-    when(gives_c, core_c.start)
+
+    @pl.when(gives_c)
+    def _():
+        for turn in range(4):
+            core_part(turn).start()
 
     @pl.when(is_a)
     def _():
-        @pl.when(y == 3)
-        def _():
-            d_sent.start()
         core_d.wait_recv()
 
         @pl.when(y == 3)
         def _():
             def columns(n):
                 u_out[n] = dot_nn(dbuf[1], wt[0, :, block(n)]).astype(BF)
-                remote(u_out.at[n], u_in.at[n], u_send.at[0], u_recv, (5, sp)).start()
+                remote(u_out.at[n], u_in.at[n], u_send.at[0], u_recv.at[n], (5, sp)).start()
             loop(4, columns)
+            d_sent.start()
 
         @pl.when(y == 2)
         def _():
-            d_sent.wait_recv()
-            u_sent.wait_recv()
-            odd = sp % 2
+            total = None
             for n in range(4):
-                x2[pl.ds(pl.multiple_of(R * odd, R), R), 256 * n:256 * (n + 1)] = u_in[n]
-            x2[pl.ds(pl.multiple_of(R * (1 - odd), R), R), :] = d_in[...]
-            x2[...] = dot_nn(x2[...], wt[1]).astype(BF)
-            core_c.wait_recv()
-            exchange(1, paired(product_chunk(0)), 7)
-        set_x(x2, dbuf[1])
-        set_x(x3, dbuf[0])
-        exchange(0, paired(level_chunk))
+                u_arrive(n)
+                term = dot_nn(u_in[n], wt[1, block(n), :])
+                total = term if total is None else total + term
+            set_x(x2, total.astype(BF))
+            turns = iter(range(4))
+
+            def chunk(q):
+                core_part(next(turns)).wait_recv()
+                return product_chunk(0)(q)
+            exchange(1, packed(chunk), 7, True)
+        @pl.when(y != 2)
+        def _():
+            set_x(x2, dbuf[1])
+            set_x(x3, dbuf[0])
+            exchange(0, paired(level_chunk))
         send_positions()
         when(y == 2, lambda: transpose_w(0, 0))
 
-        @pl.when(y < 2)
-        def _():
-            core_c.wait_recv()
-            w[2, block(quarter), :] = dot_nn(w[0, block(quarter), :], w[1]).astype(BF)
-
-            @pl.when(y == 1)
-            def _():
-                for k in range(4):
-                    part(2, k).start()
-        collect(0, True)
+        when(y < 2, core_c_here)
 
         @pl.when(y != 2)
         def _():
+            collect(0, True)
             e = (dot_nn(zbuf[0:R], wt[0]) + zbuf[R:2 * R].astype(F32)).astype(BF)
             for n in range(4):
                 state[n] = e[:, 256 * n:256 * (n + 1)]
@@ -306,12 +326,15 @@
 
         @pl.when(y == 2)
         def _():
+            collect(0, True, SP)
             vterm[...] = zbuf[...].astype(F32)
-            make_perm()
-            shifted(0).wait_recv()
+            collect(2, False, SP, True)
+            total = vterm[0:R]
             for n in range(4):
-                x2[0:R, 256 * n:256 * (n + 1)] = arrived[n]
-            x2[R:2 * R] = (dot_nn(x2[0:R], wt[1]) + vterm[0:R]).astype(BF)
+                arrive(n)
+                t = (arrived[n].astype(F32) + zbuf[0:R, block(n)].astype(F32)).astype(BF)
+                total = total + dot_nn(t, wt[1, block(n), :])
+            x2[R:2 * R] = total.astype(BF)
 
             def third(n):
                 state[n] = (dot_nn(x2[R:2 * R], wt[0, :, block(n)]) + vterm[R:2 * R, block(n)]).astype(BF)
@@ -320,16 +343,15 @@
             for k, device in ((1, 2), (2, 3)):
                 for n in range(4):
                     shift(n, k, arrived, shift_recv, device).start()
-        when(y != 2, make_perm)
+        make_perm()
         set_x_blocks(state)
         exchange(3, packed(transpose_chunk, perm_chunk))
 
         @pl.when(y < 2)
         def _():
-            def rest(d):
-                q = (quarter + 1 + d) % 4
+            def rows(q):
                 w[2, block(q), :] = dot_nn(w[0, block(q), :], w[1]).astype(BF)
-            loop(3, rest)
+            loop(4, rows)
             transpose_w(1, 2)
             make_wp(2)
         collect(3)
@@ -348,38 +370,46 @@
 
     @pl.when(is_b & (y < 3))
     def _():
+        @pl.when(y == 2)
+        def _():
+            core_d.wait_recv()
+            set_x(x2, dbuf[1])
+            set_x(x3, dbuf[0])
+            exchange(0, paired(level_chunk), 5)
         send_positions()
+        send_rows(dbuf[1])
+
+        @pl.when(y == 1)
+        def _():
+            core_q.wait_recv()
+            w[2, block(quarter), :] = dot_nn(w[0, block(quarter), :], w[1]).astype(BF)
+            for k in range(4):
+                part(2, k).start()
+        eterm[0:R] = dbuf[1].astype(F32)
 
         @pl.when(y == 2)
         def _():
-            core_d.wait_recv()
+            core_c_here()
+            transpose_w(1, 1)
+            d_sent.wait_recv()
+            set_x(x2, dot_nn(d_in[...], wt[1]).astype(BF))
+            exchange(1, packed(product_chunk(0)), 5, True, 2)
+        make_perm()
+        for k in range(4):
+            when(y == 0, lambda: share(k))
+            wp[block(k), :] = dot_nn(perm[block(k), :], w[1]).astype(BF)
+        collect_rows(eterm)
+
+    @pl.when(is_b & (y == 3))
+    def _():
         send_rows(dbuf[1])
-        eterm[0:R] = dbuf[1].astype(F32)
-
-        @pl.when(y == 2)
-        def _():
-            core_c.wait_recv()
-            transpose_w(1, 1)
-        make_perm()
-        make_wp(1)
-        collect_rows(eterm)
-
-        @pl.when(y == 0)
-        def _():
-            for k in range(4):
-                share(k)
-
-    @pl.when(is_b & (y == 3))
-    def _():
-        send_rows(dbuf[1])
-        core_c.wait_recv()
+        core_c_here()
         transpose_w(0, 0)
         final[0:R] = dbuf[1]
         collect_rows(final)
-        collect(1, True, SP)
-        t = (dot_nn(zbuf[0:R], wt[0]) + zbuf[R:2 * R].astype(F32)).astype(BF)
+        collect(1, False, SP, True)
         for n in range(4):
-            state[n] = t[:, 256 * n:256 * (n + 1)]
+            state[n] = dot_nn(zbuf[0:R], wt[0, :, block(n)]).astype(BF)
             shift(n, 0, arrived, shift_recv, 5).start()
 
     slot = jnp.where(is_a, 2, 1)
@@ -389,7 +419,7 @@
     def _():
         @pl.when(is_b)
         def _():
-            u_sent.wait_recv()
+            loop(4, u_arrive)
             give_u.start()
 
         @pl.when(is_a)
@@ -406,15 +436,14 @@
 
     @pl.when(ends)
     def _():
-        @pl.when((y > 0) | is_b)
-        def _():
-            shifted(0).wait_recv()
-
         @pl.when((y == 0) & is_b)
         def _():
+            total = None
             for n in range(4):
-                x3[0:R, 256 * n:256 * (n + 1)] = arrived[n]
-            d_in[...] = dot_nn(x3[0:R], wt[2]).astype(BF)
+                arrive(n)
+                term = dot_nn(arrived[n], wt[2, block(n), :])
+                total = term if total is None else total + term
+            d_in[...] = total.astype(BF)
             give_v.start()
             set_x(x2, d_in[...])
 
@@ -425,6 +454,7 @@
 
         @pl.when(y > 0)
         def _():
+            loop(4, arrive)
             set_x_blocks(arrived)
         exchange(2, packed(product_chunk(slot), wp_chunk))
 
@@ -471,9 +501,11 @@
     when((y == 0) & is_b, copy_core.wait_send)
     when(is_b, rows_sent.wait_send)
     when(is_a | (y < 3), positions.wait_send)
-    when(is_a, exchanged(0).wait_send)
+    when(is_a & (y != 2), exchanged(0).wait_send)
+    when(is_b & (y == 2), exchanged(0, SP).wait_send)
+    when(is_b & (y == 2), exchanged(1, SP, True).wait_send)
     when(y == 0, exchanged(1).wait_send)
-    when(is_a & (y == 2), exchanged(1, SP).wait_send)
+    when(is_a & (y == 2), exchanged(1, SP, True).wait_send)
     when(ends, exchanged(2).wait_send)
     when(is_a, exchanged(3).wait_send)
     when((is_a & (y > 0)) | (is_b & (y == 3)), shifted(0).wait_send)
@@ -483,7 +515,8 @@
     when(is_b & (y == 0), give_u.wait_send)
     when(is_a & (y == 3), u_sent.wait_send)
     when(is_a & (y == 3), d_sent.wait_send)
-    when(is_a & (y == 1), parts_sent(0).wait_send)
+    when(is_b & (y == 1), parts_sent(0).wait_send)
+    when(is_a & (y == 1), core_q.wait_send)
     when(is_b & (y == 0), shared.wait_send)
 
 
@@ -525,8 +558,8 @@
             pltpu.VMEM((4, SP, 2, 32, 128), BF),
             pltpu.VMEM((SP, 16, 256), BF),
             pltpu.VMEM((SP, 16, 256), BF),
-            dma((5,)), dma((3,)), dma((3,)), dma((4,)), dma, dma((2,)), dma, dma, dma((4,)), dma((4,)),
-            dma, dma, dma, dma, dma, dma, dma, dma((4,)), dma, dma,
+            dma((5,)), dma((3,)), dma((3,)), dma((4,)), dma((4,)), dma((2,)), dma((4,)), dma, dma((4,)), dma((4,)),
+            dma, dma, dma, dma, dma, dma, dma, dma((4,)), dma, dma, dma((4,)),
         ],
         compiler_params=pltpu.CompilerParams(
             collective_id=0, has_side_effects=True, vmem_limit_bytes=48 << 20),

time: 39.1 us -> 37.6 us (0.962)
  Pallas kernels: 36.5 us -> 35 us
    pallas_call x1, Pallas kernels: 36.5 us -> 35 us  [on_device(): pl.pallas_call(kernel, out_shape=(jax.ShapeDtypeStruct((R, N), BF), jax.S...]
where the time goes in v5:
time: 37.6 us; the launch traced here: 36.9 us
  Pallas kernels  35 us (93%)
  local copies, waits for them, and re-layouts  1.29 us (3%)
  between operations  0.64 us (2%)
    pallas_call x1, Pallas kernels, on_device(): pl.pallas_call(kernel, out_shape=(jax.ShapeDtypeStruct((R, N), BF), jax.S...  35 us
    unnamed x2, local copies, waits for them, and re-layouts  1.29 us

profile of v5, /device:TPU:1, one launch (start us, length us, event | category | flops | bytes accessed | tf_op | source)
XLA Modules:
  0.0 36.9 jit_solution(12054056083129226089)
XLA Ops:
  0.6 35.0 %selected_inverse.1 = (bf16[64,1024]{1,0:T(8,128)(2,1)S(1)}, bf16[64,512]{1,0:T(8,128)(2,1)S(1)}) custom-call(bf16[64,1024]{1,0:T(8,128)(2,1)} %bitcast.8, bf16[1024,1024]{1,0:T(8,128)(2,1)} %bitcast.7, s32[1,64]{1,0:T(1,128)} %bitcast.9, s32[1,4]{1,0:T(1,128)} %pattern_ref.1, bf16[1024,512]{1,0:T(8,128)(2,1)} %basis_ref.1), custom_call_target="tpu_custom_call" | custom-call | tf_op jit(solution)/shard_map/selected_inverse/pallas_call | solution.py:529
  35.6 0.7 %copy.9 = bf16[1,64,1024]{2,1,0:T(8,128)(2,1)} copy(bf16[1,64,1024]{2,1,0:T(8,128)(2,1)S(1)} %bitcast.5) | data formatting | bytes 262144
  36.3 0.6 %copy.10 = bf16[1,64,512]{2,1,0:T(8,128)(2,1)} copy(bf16[1,64,512]{2,1,0:T(8,128)(2,1)S(1)} %bitcast.6) | data formatting | bytes 131072

commit v6 on v5

--- a/solution.py
+++ b/solution.py
@@ -12,6 +12,9 @@
 F32 = jnp.float32
 BF = jnp.bfloat16
 FAR_FIRST = (10, 6, 14, 2, 9, 11, 5, 7, 13, 15, 1, 3, 8, 4, 12)
+
+ONE_TO_ONE = ((1, 0), (2, 1), (2, 3), (3, 1), (3, 2), (5, 1), (5, 2), (5, 3), (5, 4), (6, 4), (6, 5), (7, 5), (7, 6))
+ALL_TO_ALL = tuple((t, t) for t in range(7)) + ((4, 5), (5, 7), (6, 7))
 
 
 def dot_nt(a, b):
@@ -59,7 +62,7 @@
     load_p = pltpu.make_async_copy(pos_ref, pos, local_sem.at[2])
     load_t = pltpu.make_async_copy(pattern_ref, pattern, local_sem.at[3])
     load_b = pltpu.make_async_copy(basis_ref, basis, local_sem.at[4])
-    for load in (load_c, load_d, load_p, load_t, load_b):
+    for load in (load_d, load_c, load_p, load_t, load_b):
         load.start()
 
     barrier = pltpu.get_barrier_semaphore()
@@ -67,18 +70,18 @@
     def greet(t, s):
         pl.semaphore_signal(barrier, inc=1, device_id=(t, s), device_id_type=MESH)
 
-    for d in FAR_FIRST:
-        greet(tm, (sp + d) % SP)
-    for dy in (2, 1, 3):
-        for core in (0, 1):
-            greet(((y + dy) % 4) * 2 + core, sp)
-    greet(*partner)
-
-    for left, right in ((4, 5), (5, 7)):
-        @pl.when((tm == left) | (tm == right))
-        def _():
-            for d in FAR_FIRST:
-                greet(left + right - tm, (sp + d) % SP)
+    for t in range(8):
+        @pl.when(tm == t)
+        def _():
+            for source, to in ALL_TO_ALL:
+                if to == t:
+                    for d in FAR_FIRST + ((0,) if source != to else ()):
+                        greet(source, (sp + d) % SP)
+            for source, to in ONE_TO_ONE:
+                if to == t:
+                    greet(source, sp)
+    greets = sum(jnp.where(tm == t, sum(SP - (a == b) for a, b in ALL_TO_ALL if a == t) + sum(a == t for a, _ in ONE_TO_ONE), 0)
+                 for t in range(8))
 
     lane = lax.broadcasted_iota(jnp.int32, (1, 1, 128), 2)
     low = lane < R
@@ -92,16 +95,29 @@
     def transpose_w(to, slot):
         loop(4, lambda p: wt.__setitem__((to, slice(None), block(p)), w[slot, block(p), :].T))
 
+    core_d = remote(dbuf.at[c], dbuf.at[c], core_send.at[0], core_recv.at[0], partner)
+    load_d.wait()
+
+    @pl.when(tm == 7)
+    def _():
+        pl.semaphore_wait(barrier, greets)
+        core_d.start()
     load_c.wait()
     when((c == 0) & (y != 2), lambda: transpose_w(0, 0))
     when((c == 1) & (y < 3), lambda: transpose_w(1, 1))
-    load_d.wait()
     load_p.wait()
     load_t.wait()
-    crossings = jnp.where(tm == 5, 2, jnp.where((tm == 4) | (tm == 7), 1, 0))
-    pl.semaphore_wait(barrier, SP + 6 + (SP - 1) * crossings)
-
-    core_d = remote(dbuf.at[c], dbuf.at[c], core_send.at[0], core_recv.at[0], partner)
+
+    @pl.when(tm == 6)
+    def _():
+        core_d.wait_recv()
+        for n in range(4):
+            u_out[n] = dot_nn(dbuf[1], wt[0, :, block(n)]).astype(BF)
+
+    @pl.when(tm != 7)
+    def _():
+        pl.semaphore_wait(barrier, greets)
+
     core_c = remote(w.at[c], w.at[c], core_send.at[1], core_recv.at[1], partner)
 
     def core_part(turn):
@@ -224,7 +240,7 @@
     def make_wp(slot):
         loop(4, lambda p: wp.__setitem__((block(p), slice(None)), dot_nn(perm[block(p), :], w[slot]).astype(BF)))
 
-    def send_rows(value):
+    def send_rows(value, to=None):
         position = pos[...]
         target = position // R * 4 + position % 4
         place = (lax.broadcasted_iota(jnp.int32, (R, R), 0) == target).astype(BF)
@@ -234,13 +250,17 @@
         rows_out[...] = dot_nn(spread, stacked).astype(BF).reshape(SP, 16, 256)
         for d in FAR_FIRST:
             i = (sp + d) % SP
-            remote(rows_out.at[i], rows_in.at[sp], rows_send, rows_recv, (tm, i)).start()
-        rows_in[pl.ds(sp, 1)] = rows_out[pl.ds(sp, 1)]
-
-    rows_sent = remote(rows_out.at[pl.ds(0, SP - 1)], rows_in.at[pl.ds(0, SP - 1)], rows_send, rows_recv, partner)
-
-    def collect_rows(ref):
-        rows_sent.wait_recv()
+            remote(rows_out.at[i], rows_in.at[sp], rows_send, rows_recv, (tm if to is None else to, i)).start()
+        if to is None:
+            rows_in[pl.ds(sp, 1)] = rows_out[pl.ds(sp, 1)]
+        else:
+            remote(rows_out.at[sp], rows_in.at[sp], rows_send, rows_recv, (to, sp)).start()
+
+    def rows_sent(count=SP - 1):
+        return remote(rows_out.at[pl.ds(0, count)], rows_in.at[pl.ds(0, count)], rows_send, rows_recv, partner)
+
+    def collect_rows(ref, count=SP - 1):
+        rows_sent(count).wait_recv()
         gather = (ci == (ri % R) // 4 * 16 + ri // R * 4 + ri % 4).astype(BF)
         own = dot_nn(gather, rows_in[...].reshape(256, 256))
         for k in range(4):
@@ -264,7 +284,7 @@
     give_u = remote(u_in, u_in, u_send.at[0], u_recv.at[0], partner)
     give_v = remote(d_in, d_in, u_send.at[1], d_recv, partner)
     when(is_a & (y == 1), core_q.start)
-    when(gives_d, core_d.start)
+    when(gives_d & (tm != 7), core_d.start)
 
     @pl.when(gives_c)
     def _():
@@ -273,12 +293,11 @@
 
     @pl.when(is_a)
     def _():
-        core_d.wait_recv()
+        when(y != 3, core_d.wait_recv)
 
         @pl.when(y == 3)
         def _():
             def columns(n):
-                u_out[n] = dot_nn(dbuf[1], wt[0, :, block(n)]).astype(BF)
                 remote(u_out.at[n], u_in.at[n], u_send.at[0], u_recv.at[n], (5, sp)).start()
             loop(4, columns)
             d_sent.start()
@@ -304,6 +323,7 @@
             exchange(0, paired(level_chunk))
         send_positions()
         when(y == 2, lambda: transpose_w(0, 0))
+        when(y == 3, lambda: send_rows(dbuf[1], 7))
 
         when(y < 2, core_c_here)
 
@@ -402,11 +422,10 @@
 
     @pl.when(is_b & (y == 3))
     def _():
-        send_rows(dbuf[1])
         core_c_here()
         transpose_w(0, 0)
         final[0:R] = dbuf[1]
-        collect_rows(final)
+        collect_rows(final, SP)
         collect(1, False, SP, True)
         for n in range(4):
             state[n] = dot_nn(zbuf[0:R], wt[0, :, block(n)]).astype(BF)
@@ -464,22 +483,20 @@
             def _():
                 copy_core.wait_recv()
                 transpose_w(2, 3)
+            loop(4, lambda k: wt.__setitem__((0, block(k)), dot_nn(wt[2, block(k), :], wt[1]).astype(BF)))
             collect(1)
-            vterm[...] = zbuf[...].astype(F32)
+            eterm[...] = eterm[...] + dot_nn(zbuf[...], wt[1])
         collect(2)
 
         @pl.when(y == 0)
         def _():
-            zbuf[...] = (dot_nn(zbuf[...], wt[2]) + vterm[...]).astype(BF)
-        out = (eterm[...] + dot_nn(zbuf[...], wt[1])).astype(BF)
-
-        @pl.when(y < 2)
-        def _():
-            final[...] = out
-
-        @pl.when(y == 2)
-        def _():
-            sent_final[...] = out
+            final[...] = (eterm[...] + dot_nn(zbuf[...], wt[0])).astype(BF)
+
+        @pl.when(y > 0)
+        def _():
+            out = (eterm[...] + dot_nn(zbuf[...], wt[1])).astype(BF)
+            when(y == 1, lambda: final.__setitem__(Ellipsis, out))
+            when(y == 2, lambda: sent_final.__setitem__(Ellipsis, out))
 
     @pl.when(y == 2)
     def _():
@@ -499,7 +516,8 @@
     when(gives_d, core_d.wait_send)
     when(gives_c, core_c.wait_send)
     when((y == 0) & is_b, copy_core.wait_send)
-    when(is_b, rows_sent.wait_send)
+    when(is_b & (y < 3), rows_sent().wait_send)
+    when(is_a & (y == 3), rows_sent(SP).wait_send)
     when(is_a | (y < 3), positions.wait_send)
     when(is_a & (y != 2), exchanged(0).wait_send)
     when(is_b & (y == 2), exchanged(0, SP).wait_send)

time: 37.6 us -> 35.8 us (0.952)
  the two profiles are of different devices: /device:TPU:1 before, /device:TPU:0 now
where the time goes in v6:
time: 35.8 us; the launch traced here: 35.7 us
  Pallas kernels  33.8 us (94%)
  local copies, waits for them, and re-layouts  1.29 us (4%)
  between operations  0.64 us (2%)
    pallas_call x1, Pallas kernels, on_device(): pl.pallas_call(kernel, out_shape=(jax.ShapeDtypeStruct((R, N), BF), jax.S...  33.8 us
    unnamed x2, local copies, waits for them, and re-layouts  1.29 us

profile of v6, /device:TPU:0, one launch (start us, length us, event | category | flops | bytes accessed | tf_op | source)
XLA Modules:
  0.0 35.7 jit_solution(17209411461292544242)
XLA Ops:
  0.6 33.8 %selected_inverse.1 = (bf16[64,1024]{1,0:T(8,128)(2,1)S(1)}, bf16[64,512]{1,0:T(8,128)(2,1)S(1)}) custom-call(bf16[64,1024]{1,0:T(8,128)(2,1)} %bitcast.8, bf16[1024,1024]{1,0:T(8,128)(2,1)} %bitcast.7, s32[1,64]{1,0:T(1,128)} %bitcast.9, s32[1,4]{1,0:T(1,128)} %pattern_ref.1, bf16[1024,512]{1,0:T(8,128)(2,1)} %basis_ref.1), custom_call_target="tpu_custom_call" | custom-call | tf_op jit(solution)/shard_map/selected_inverse/pallas_call | solution.py:547
  34.4 0.7 %copy.9 = bf16[1,64,1024]{2,1,0:T(8,128)(2,1)} copy(bf16[1,64,1024]{2,1,0:T(8,128)(2,1)S(1)} %bitcast.5) | data formatting | bytes 262144
  35.1 0.6 %copy.10 = bf16[1,64,512]{2,1,0:T(8,128)(2,1)} copy(bf16[1,64,512]{2,1,0:T(8,128)(2,1)S(1)} %bitcast.6) | data formatting | bytes 131072

commit v7 on v6

--- a/solution.py
+++ b/solution.py
@@ -13,7 +13,7 @@
 BF = jnp.bfloat16
 FAR_FIRST = (10, 6, 14, 2, 9, 11, 5, 7, 13, 15, 1, 3, 8, 4, 12)
 
-ONE_TO_ONE = ((1, 0), (2, 1), (2, 3), (3, 1), (3, 2), (5, 1), (5, 2), (5, 3), (5, 4), (6, 4), (6, 5), (7, 5), (7, 6))
+ONE_TO_ONE = ((1, 0), (2, 0), (2, 1), (2, 3), (3, 1), (3, 2), (5, 1), (5, 2), (5, 3), (5, 4), (6, 4), (6, 5), (7, 5), (7, 6))
 ALL_TO_ALL = tuple((t, t) for t in range(7)) + ((4, 5), (5, 7), (6, 7))
 
 
@@ -129,6 +129,10 @@
             core_part(turn).wait_recv()
 
     copy_core = remote(w.at[3], w.at[3], core_send.at[2], core_recv.at[2], partner)
+
+    def copy_rows(rows):
+        return remote(w.at[3, rows], w.at[3, rows], core_send.at[2], core_recv.at[2], partner)
+
     core_q = remote(w.at[0, block(quarter)], w.at[0, block(quarter)], core_send.at[2], core_recv.at[2], partner)
     gives_d = (c == 1) | (y == 2)
     gives_c = ((c == 1) & (y < 3)) | ((c == 0) & (y > 1))
@@ -143,6 +147,7 @@
     def share(k):
         part(3, k).wait_recv()
         first = 256 * quarter + 64 * k
+        copy_rows(pl.ds(pl.multiple_of(first, 64), 64)).start()
         xs, zs = ((xc + 1) % 4, (xc + 3) % 4), ((zc + 1) % 4, (zc + 3) % 4)
         to = [(4 * zs[0] + xs[0], 0, 16), (4 * zs[0] + xs[1], 16, 16), (4 * zs[1] + xs[0], 32, 16), (4 * zs[1] + xs[1], 48, 16),
               (4 * zc + xs[0], 0, 32), (4 * zc + xs[1], 32, 32), (4 * zs[0] + xc, 0, 32), (4 * zs[1] + xc, 32, 32)]
@@ -281,7 +286,6 @@
     u_sent = remote(u_out, u_in, u_send.at[0], u_recv.at[0], (5, sp))
     d_sent = remote(dbuf.at[0], d_in, u_send.at[1], d_recv, (4, sp))
 
-    give_u = remote(u_in, u_in, u_send.at[0], u_recv.at[0], partner)
     give_v = remote(d_in, d_in, u_send.at[1], d_recv, partner)
     when(is_a & (y == 1), core_q.start)
     when(gives_d & (tm != 7), core_d.start)
@@ -341,8 +345,9 @@
 
             @pl.when(y == 1)
             def _():
-                for n in range(4):
-                    shift(n, 0, u_in, u_recv, 1).start()
+                for core in (0, 1):
+                    for n in range(4):
+                        shift(n, core, u_in, u_recv, core).start()
 
         @pl.when(y == 2)
         def _():
@@ -374,19 +379,11 @@
             loop(4, rows)
             transpose_w(1, 2)
             make_wp(2)
-        collect(3)
-
-        @pl.when(y < 2)
-        def _():
-            eterm[...] = zbuf[...].astype(F32)
-
-        @pl.when(y == 2)
-        def _():
-            sent_final[...] = zbuf[...]
-
-        @pl.when(y == 3)
-        def _():
-            final[...] = zbuf[...]
+        @pl.when(y > 1)
+        def _():
+            collect(3)
+            when(y == 2, lambda: sent_final.__setitem__(Ellipsis, zbuf[...]))
+            when(y == 3, lambda: final.__setitem__(Ellipsis, zbuf[...]))
 
     @pl.when(is_b & (y < 3))
     def _():
@@ -436,21 +433,15 @@
 
     @pl.when(y == 0)
     def _():
-        @pl.when(is_b)
-        def _():
-            loop(4, u_arrive)
-            give_u.start()
-
-        @pl.when(is_a)
-        def _():
-            give_u.wait_recv()
+        loop(4, u_arrive)
         set_x_blocks(u_in)
         exchange(1, packed(product_chunk(slot), wp_chunk))
 
         @pl.when(is_b)
         def _():
             shared.wait_recv()
-            copy_core.start()
+            for d in (1, 2, 3):
+                copy_rows(block((quarter + d) % 4)).start()
             transpose_w(2, 3)
 
     @pl.when(ends)
@@ -476,6 +467,11 @@
             loop(4, arrive)
             set_x_blocks(arrived)
         exchange(2, packed(product_chunk(slot), wp_chunk))
+
+        @pl.when(is_a)
+        def _():
+            collect(3)
+            eterm[...] = zbuf[...].astype(F32)
 
         @pl.when(y == 0)
         def _():
@@ -527,10 +523,9 @@
     when(ends, exchanged(2).wait_send)
     when(is_a, exchanged(3).wait_send)
     when((is_a & (y > 0)) | (is_b & (y == 3)), shifted(0).wait_send)
-    when(is_a & (y == 2), shifted(1).wait_send)
+    when(is_a & ((y == 1) | (y == 2)), shifted(1).wait_send)
     when(is_a & (y == 2), shifted(2).wait_send)
     when(is_b & (y == 0), give_v.wait_send)
-    when(is_b & (y == 0), give_u.wait_send)
     when(is_a & (y == 3), u_sent.wait_send)
     when(is_a & (y == 3), d_sent.wait_send)
     when(is_b & (y == 1), parts_sent(0).wait_send)

time: 35.8 us -> 35.6 us (level)
  the two profiles are of different devices: /device:TPU:0 before, /device:TPU:1 now
where the time goes in v7:
time: 35.6 us; the launch traced here: 35 us
  Pallas kernels  33.1 us (93%)
  local copies, waits for them, and re-layouts  1.29 us (4%)
  between operations  0.64 us (2%)
    pallas_call x1, Pallas kernels, on_device(): pl.pallas_call(kernel, out_shape=(jax.ShapeDtypeStruct((R, N), BF), jax.S...  33.1 us
    unnamed x2, local copies, waits for them, and re-layouts  1.29 us

profile of v7, /device:TPU:1, one launch (start us, length us, event | category | flops | bytes accessed | tf_op | source)
XLA Modules:
  0.0 35.0 jit_solution(3930462446357800391)
XLA Ops:
  0.6 33.1 %selected_inverse.1 = (bf16[64,1024]{1,0:T(8,128)(2,1)S(1)}, bf16[64,512]{1,0:T(8,128)(2,1)S(1)}) custom-call(bf16[64,1024]{1,0:T(8,128)(2,1)} %bitcast.8, bf16[1024,1024]{1,0:T(8,128)(2,1)} %bitcast.7, s32[1,64]{1,0:T(1,128)} %bitcast.9, s32[1,4]{1,0:T(1,128)} %pattern_ref.1, bf16[1024,512]{1,0:T(8,128)(2,1)} %basis_ref.1), custom_call_target="tpu_custom_call" | custom-call | tf_op jit(solution)/shard_map/selected_inverse/pallas_call | solution.py:542
  33.7 0.7 %copy.9 = bf16[1,64,1024]{2,1,0:T(8,128)(2,1)} copy(bf16[1,64,1024]{2,1,0:T(8,128)(2,1)S(1)} %bitcast.5) | data formatting | bytes 262144
  34.3 0.6 %copy.10 = bf16[1,64,512]{2,1,0:T(8,128)(2,1)} copy(bf16[1,64,512]{2,1,0:T(8,128)(2,1)S(1)} %bitcast.6) | data formatting | bytes 131072
